TPU v7x, 32 devices: a whole 2x2x4 slice. The times are simulated.
32 devices in a mesh: pipe: 4 (over x, core), wide: 8 (over z, y).
Axes of the slice: x: 2, y: 2, z: 4, core: 2. Of those that a mesh axis runs over, the one named last changes fastest.
Arguments:
- page_tokens: bfloat16 [24, 40, 20, 512], P('wide'), may hold values from -6 to 6
- blank: int32 [24, 200], P('wide'), may hold values 0 or 1
- cotangent: bfloat16 [24, 200, 1024], P('wide'), may hold values from -6 to 6
- first: bfloat16 [4, 1024, 4096], P('pipe')
- second: bfloat16 [4, 4096, 1024], P('pipe'), may hold values from -0.09375 to 0.09375
- gains: float32 [4, 3, 1024], P('pipe'), may hold values from 0.5 to 1.5
- biases: float32 [4, 6, 1024], P('pipe'), may hold values from -1 to 1
- tables: float32 [2, 32, 361], replicated, may hold values from -4 to 4
Outputs:
- output: bfloat16 [24, 200, 1024], P('wide', None, 'pipe')
- input_grad: float32 [24, 40, 20, 512], P('wide', None, None, 'pipe')
- first_grad: float32 [4, 1024, 4096], P('pipe', 'wide')
- second_grad: float32 [4, 4096, 1024], P('pipe', None, 'wide')
- gains_grad: float32 [4, 3, 1024], P('pipe', None, 'wide')
- biases_grad: float32 [4, 6, 1024], P('pipe', None, 'wide')
- tables_grad: float32 [2, 32, 361], replicated
Inputs may be any that keep to these rules, and one draw needn't show every extreme that they name: 1 marks a blank cell.
All inputs are finite; a program needn't handle non-finite values. No bound on the sum of `blank` on one device may be relied on, other than what follows from the above.
Results may differ from a plain program's by a relative error of at most 0.024.
Values may be sent and summed in bfloat16 or wider, within the bound.
A program may use at most 320 MiB of HBM per device.

v0:
```python
import jax
import jax.numpy as jnp
from jax import lax
from jax.sharding import PartitionSpec as P

HEADS = 32
WIN = 10
GRID_H = 20
GRID_W = 10


EPSILON = 1e-05
NEGATIVE = -1000000000.0


def shifted_2(array, axis, by):
    size = lax.axis_size(axis)
    pairs = [(i, i + by) for i in range(size) if 0 <= i + by < size]
    return lax.ppermute(array, axis, pairs)


def norm_forward(values, gain_row, shift_row):
    average = jnp.mean(values, -1, keepdims=True)
    centered = values - average
    inv_std = lax.rsqrt(jnp.mean(centered * centered, -1, keepdims=True) + EPSILON)
    unit_norm = centered * inv_std
    return (unit_norm * gain_row + shift_row, unit_norm, inv_std)


def norm_backward(grad_out, unit_norm, inv_std, gain_row):
    scaled = grad_out * gain_row
    grad_in = inv_std * (
        scaled
        - jnp.mean(scaled, -1, keepdims=True)
        - unit_norm * jnp.mean(scaled * unit_norm, -1, keepdims=True)
    )
    return (grad_in, jnp.sum(grad_out * unit_norm, 0), jnp.sum(grad_out, 0))


def gelu(values):
    return 0.5 * values * (1.0 + lax.erf(values * 0.7071067811865476))


def gelu_slope(values):
    return (
        0.5 * (1.0 + lax.erf(values * 0.7071067811865476))
        + values * jnp.exp(-0.5 * values * values) * 0.3989422804014327
    )


def outer_sum(left, right):
    return lax.dot_general(
        left, right, (((0,), (0,)), ((), ())), preferred_element_type=jnp.float32
    )


def back_dot(grad_rows, weight):
    return lax.dot_general(
        grad_rows, weight, (((1,), (1,)), ((), ())), preferred_element_type=jnp.float32
    )


def merge_tokens(tokens):
    channels = tokens.shape[-1]
    grid = tokens.reshape(GRID_H, 2, GRID_W, 2, channels)
    grid = jnp.transpose(grid, (0, 2, 3, 1, 4))
    return grid.reshape(GRID_H * GRID_W, 4 * channels)


def unmerge_tokens(merged):
    channels = merged.shape[-1] // 4
    grid = merged.reshape(GRID_H, GRID_W, 2, 2, channels)
    grid = jnp.transpose(grid, (0, 3, 1, 2, 4))
    return grid.reshape(2 * GRID_H, 2 * GRID_W, channels)


def to_windows(values):
    channels = values.shape[-1]
    grid = values.reshape(GRID_H // WIN, WIN, GRID_W // WIN, WIN, channels)
    return jnp.transpose(grid, (0, 2, 1, 3, 4)).reshape(GRID_H * GRID_W, channels)


def from_windows(values):
    channels = values.shape[-1]
    grid = values.reshape(GRID_H // WIN, GRID_W // WIN, WIN, WIN, channels)
    return jnp.transpose(grid, (0, 2, 1, 3, 4)).reshape(GRID_H * GRID_W, channels)


def roll_grid(values, amount):
    channels = values.shape[-1]
    grid = values.reshape(GRID_H, GRID_W, channels)
    return jnp.roll(grid, (amount, amount), (0, 1)).reshape(GRID_H * GRID_W, channels)


def window_blank(blank_row, shifted):
    marks = blank_row[:, None]
    if shifted:
        marks = roll_grid(marks, -(WIN // 2))
    return to_windows(marks)[:, 0]


def region_ids(shifted):
    cells = jnp.arange(GRID_H * GRID_W)
    rows_at = cells // GRID_W
    cols_at = cells % GRID_W
    if shifted:
        row_band = (rows_at >= GRID_H - WIN).astype(jnp.int32) + (
            rows_at >= GRID_H - WIN // 2
        ).astype(jnp.int32)
        col_band = (cols_at >= GRID_W - WIN).astype(jnp.int32) + (
            cols_at >= GRID_W - WIN // 2
        ).astype(jnp.int32)
        region = row_band * 3 + col_band
    else:
        region = jnp.zeros_like(rows_at)
    return to_windows(region.reshape(-1, 1))[:, 0]


def window_mask(key_blank, shifted):
    area = WIN * WIN
    window_count = key_blank.shape[0] // area
    region = region_ids(shifted).reshape(window_count, area)
    same_region = region[:, :, None] == region[:, None, :]
    open_key = key_blank.reshape(window_count, 1, area) == 0
    own_key = jnp.eye(area, dtype=jnp.bool_)[None]
    return (same_region & (open_key | own_key))[:, None]


def relative_onehot():
    span = 2 * WIN - 1
    cells = jnp.arange(WIN * WIN)
    rows_at = cells // WIN
    cols_at = cells % WIN
    offsets = (rows_at[:, None] - rows_at[None, :] + WIN - 1) * span + (
        cols_at[:, None] - cols_at[None, :] + WIN - 1
    )
    return (offsets.reshape(-1, 1) == jnp.arange(span * span)[None, :]).astype(jnp.float32)


def split_heads(rows):
    area = WIN * WIN
    return rows.reshape(rows.shape[0] // area, area, HEADS, rows.shape[1] // HEADS)


def join_heads(split_rows):
    return split_rows.reshape(
        split_rows.shape[0] * split_rows.shape[1], split_rows.shape[2] * split_rows.shape[3]
    )


def window_scores(queries, key_rows, table_rows, key_blank, shifted, onehot):
    area = WIN * WIN
    head_dim = queries.shape[1] // HEADS
    raw_scores = jnp.einsum(
        "wqhd,wkhd->whqk",
        split_heads(queries),
        split_heads(key_rows),
        preferred_element_type=jnp.float32,
    )
    relative = jnp.dot(
        table_rows, onehot.T, precision=lax.Precision.HIGHEST, preferred_element_type=jnp.float32
    ).reshape(HEADS, area, area)
    return jnp.where(
        window_mask(key_blank, shifted), raw_scores * head_dim ** (-0.5) + relative[None], NEGATIVE
    )


def attention_forward(stream, layer_weight, vectors, table_rows, blank_row, shifted, onehot):
    gain_row, shift_row, query_bias, value_bias, output_bias = vectors
    d_model = stream.shape[1]
    normed, unit_norm, inv_std = norm_forward(stream, gain_row, shift_row)
    normed_b = normed.astype(jnp.bfloat16)
    if shifted:
        normed_b = roll_grid(normed_b, -(WIN // 2))
    normed_b = to_windows(normed_b)
    key_blank = window_blank(blank_row, shifted)
    projected = jnp.dot(
        normed_b, layer_weight[:, : 3 * d_model], preferred_element_type=jnp.float32
    )
    queries = (projected[:, :d_model] + query_bias).astype(jnp.bfloat16)
    key_rows = projected[:, d_model : 2 * d_model].astype(jnp.bfloat16)
    value_rows = (projected[:, 2 * d_model :] + value_bias).astype(jnp.bfloat16)
    scores = window_scores(queries, key_rows, table_rows, key_blank, shifted, onehot)
    topmost = jnp.max(scores, -1, keepdims=True)
    exponent = jnp.exp(scores - topmost)
    total = jnp.sum(exponent, -1, keepdims=True)
    probs_b = (exponent / total).astype(jnp.bfloat16)
    log_total = topmost + jnp.log(total)
    mixed = jnp.einsum(
        "whqk,wkhd->wqhd", probs_b, split_heads(value_rows), preferred_element_type=jnp.float32
    )
    mixed_b = join_heads(mixed).astype(jnp.bfloat16)
    result = (
        jnp.dot(mixed_b, layer_weight[:, 3 * d_model :], preferred_element_type=jnp.float32)
        + output_bias
    )
    result = from_windows(result)
    if shifted:
        result = roll_grid(result, WIN // 2)
    packed = jnp.concatenate([queries, key_rows, value_rows, mixed_b], 1)
    return (stream + result, (unit_norm, inv_std, normed_b, packed, log_total))


def attention_backward(grad, saved, layer_weight, gain_row, table_rows, blank_row, shifted, onehot):
    unit_norm, inv_std, normed_b, packed, log_total = saved
    d_model = grad.shape[1]
    head_dim = d_model // HEADS
    queries = packed[:, :d_model]
    key_rows = packed[:, d_model : 2 * d_model]
    value_rows = packed[:, 2 * d_model : 3 * d_model]
    mixed_b = packed[:, 3 * d_model :]
    key_blank = window_blank(blank_row, shifted)
    grad_win = grad
    if shifted:
        grad_win = roll_grid(grad_win, -(WIN // 2))
    grad_win = to_windows(grad_win)
    output_bias_grad = jnp.sum(grad_win, 0)
    grad_b = grad_win.astype(jnp.bfloat16)
    out_weight_grad = outer_sum(mixed_b, grad_b)
    mixed_grad = split_heads(back_dot(grad_b, layer_weight[:, 3 * d_model :]).astype(jnp.bfloat16))
    scores = window_scores(queries, key_rows, table_rows, key_blank, shifted, onehot)
    probs = jnp.exp(scores - log_total)
    probs_b = probs.astype(jnp.bfloat16)
    prob_grad = jnp.einsum(
        "wqhd,wkhd->whqk", mixed_grad, split_heads(value_rows), preferred_element_type=jnp.float32
    )
    value_grad = join_heads(
        jnp.einsum("whqk,wqhd->wkhd", probs_b, mixed_grad, preferred_element_type=jnp.float32)
    ).astype(jnp.bfloat16)
    score_grad = probs * (prob_grad - jnp.sum(probs * prob_grad, -1, keepdims=True))
    area = WIN * WIN
    table_grad = jnp.dot(
        jnp.sum(score_grad, 0).reshape(HEADS, area * area),
        onehot,
        precision=lax.Precision.HIGHEST,
        preferred_element_type=jnp.float32,
    )
    raw_grad = (score_grad * head_dim ** (-0.5)).astype(jnp.bfloat16)
    query_grad = join_heads(
        jnp.einsum(
            "whqk,wkhd->wqhd", raw_grad, split_heads(key_rows), preferred_element_type=jnp.float32
        )
    ).astype(jnp.bfloat16)
    key_grad = join_heads(
        jnp.einsum(
            "whqk,wqhd->wkhd", raw_grad, split_heads(queries), preferred_element_type=jnp.float32
        )
    ).astype(jnp.bfloat16)
    proj_grad = jnp.concatenate([query_grad, key_grad, value_grad], 1)
    qkv_weight_grad = outer_sum(normed_b, proj_grad)
    normed_grad = from_windows(back_dot(proj_grad, layer_weight[:, : 3 * d_model]))
    if shifted:
        normed_grad = roll_grid(normed_grad, WIN // 2)
    stream_grad, gain_grad, shift_grad = norm_backward(normed_grad, unit_norm, inv_std, gain_row)
    query_bias_grad = jnp.sum(query_grad.astype(jnp.float32), 0)
    value_bias_grad = jnp.sum(value_grad.astype(jnp.float32), 0)
    weight_grad = jnp.concatenate([qkv_weight_grad, out_weight_grad], 1)
    return (
        grad + stream_grad,
        (
            weight_grad,
            gain_grad,
            shift_grad,
            query_bias_grad,
            value_bias_grad,
            output_bias_grad,
            table_grad,
        ),
    )


def mlp_forward(stream, first_rows, second_rows, vectors):
    gain_row, shift_row, inner_bias, outer_bias = vectors
    normed, unit_norm, inv_std = norm_forward(stream, gain_row, shift_row)
    normed_b = normed.astype(jnp.bfloat16)
    preact = jnp.dot(normed_b, first_rows, preferred_element_type=jnp.float32) + inner_bias
    hidden_b = gelu(preact).astype(jnp.bfloat16)
    result = jnp.dot(hidden_b, second_rows, preferred_element_type=jnp.float32) + outer_bias
    return (stream + result, (unit_norm, inv_std, normed_b, hidden_b, preact))


def local(page_tokens, blank, cotangent, first, second, gains, biases, tables):
    sections = lax.axis_size("pipe")
    section_index = lax.axis_index("pipe")
    micro_count = page_tokens.shape[0]
    first_rows = first[0]
    second_rows = second[0]
    gain_rows = gains[0]
    bias_rows = biases[0]
    d_model = first_rows.shape[0]
    hidden_width = first_rows.shape[1]
    token_count = GRID_H * GRID_W
    window_count = token_count // (WIN * WIN)
    onehot = relative_onehot()
    attn_vectors = (gain_rows[0], bias_rows[0], bias_rows[1], bias_rows[2], bias_rows[3])
    mlp_vectors = (gain_rows[0], bias_rows[0], bias_rows[1:5].reshape(-1), bias_rows[5])
    token_zero = jnp.zeros(page_tokens.shape[1:], jnp.float32)
    stream_zero = jnp.zeros((token_count, d_model), jnp.float32)
    table_zero = jnp.zeros(tables.shape[1:], jnp.float32)

    def saved_zeros():
        return (
            jnp.zeros((token_count, d_model), jnp.float32),
            jnp.zeros((token_count, 1), jnp.float32),
            jnp.zeros((token_count, d_model), jnp.bfloat16),
            jnp.zeros((token_count, hidden_width), jnp.bfloat16),
            jnp.zeros((token_count, hidden_width), jnp.float32),
            jnp.zeros((window_count, HEADS, WIN * WIN, 1), jnp.float32),
            jnp.zeros((token_count, 2 * d_model), jnp.float32),
            jnp.zeros((token_count, 1), jnp.float32),
            jnp.zeros((token_count, 2 * d_model), jnp.bfloat16),
        )

    def forward_first(stream, tokens_now, blank_now):
        merged = merge_tokens(tokens_now).astype(jnp.float32)
        merge_norm, merge_unit, merge_inv = norm_forward(
            merged, gain_rows[1:3].reshape(-1), bias_rows[4:6].reshape(-1)
        )
        merge_b = merge_norm.astype(jnp.bfloat16)
        start = jnp.dot(merge_b, second_rows[: 2 * d_model], preferred_element_type=jnp.float32)
        result, parts = attention_forward(
            start, first_rows, attn_vectors, tables[0], blank_now, False, onehot
        )
        empty = saved_zeros()
        return (
            result,
            (
                parts[0],
                parts[1],
                parts[2],
                parts[3],
                empty[4],
                parts[4],
                merge_unit,
                merge_inv,
                merge_b,
            ),
        )

    def forward_mlp(stream, tokens_now, blank_now):
        result, parts = mlp_forward(stream, first_rows, second_rows, mlp_vectors)
        empty = saved_zeros()
        return (
            result,
            (
                parts[0],
                parts[1],
                parts[2],
                parts[3],
                parts[4],
                empty[5],
                empty[6],
                empty[7],
                empty[8],
            ),
        )

    def forward_shifted(stream, tokens_now, blank_now):
        result, parts = attention_forward(
            stream, first_rows, attn_vectors, tables[1], blank_now, True, onehot
        )
        empty = saved_zeros()
        return (
            result,
            (
                parts[0],
                parts[1],
                parts[2],
                parts[3],
                empty[4],
                parts[4],
                empty[6],
                empty[7],
                empty[8],
            ),
        )

    def backward_first(saved, grad, blank_now):
        unit_norm, inv_std, normed_b, packed, wide_f, log_total, merge_unit, merge_inv, merge_b = (
            saved
        )
        start_grad, pieces = attention_backward(
            grad,
            (unit_norm, inv_std, normed_b, packed, log_total),
            first_rows,
            gain_rows[0],
            tables[0],
            blank_now,
            False,
            onehot,
        )
        (
            weight_grad,
            gain_grad,
            shift_grad,
            query_bias_grad,
            value_bias_grad,
            output_bias_grad,
            table_grad,
        ) = pieces
        start_b = start_grad.astype(jnp.bfloat16)
        merge_weight_grad = outer_sum(merge_b, start_b)
        merge_grad = back_dot(start_b, second_rows[: 2 * d_model])
        merged_grad, merge_gain_grad, merge_shift_grad = norm_backward(
            merge_grad, merge_unit, merge_inv, gain_rows[1:3].reshape(-1)
        )
        second_grad = jnp.concatenate(
            [merge_weight_grad, jnp.zeros((hidden_width - 2 * d_model, d_model), jnp.float32)], 0
        )
        gain_all = jnp.concatenate([gain_grad[None], merge_gain_grad.reshape(2, d_model)], 0)
        bias_all = jnp.concatenate(
            [
                jnp.stack([shift_grad, query_bias_grad, value_bias_grad, output_bias_grad]),
                merge_shift_grad.reshape(2, d_model),
            ],
            0,
        )
        table_all = jnp.stack([table_grad, table_zero])
        return (
            stream_zero,
            unmerge_tokens(merged_grad),
            weight_grad,
            second_grad,
            gain_all,
            bias_all,
            table_all,
        )

    def backward_mlp(saved, grad, blank_now):
        unit_norm, inv_std, normed_b, hidden_b, preact = saved[:5]
        outer_bias_grad = jnp.sum(grad, 0)
        grad_b = grad.astype(jnp.bfloat16)
        second_grad = outer_sum(hidden_b, grad_b)
        pre_grad = back_dot(grad_b, second_rows) * gelu_slope(preact)
        inner_bias_grad = jnp.sum(pre_grad, 0)
        pre_b = pre_grad.astype(jnp.bfloat16)
        first_grad = outer_sum(normed_b, pre_b)
        normed_grad = back_dot(pre_b, first_rows)
        stream_grad, gain_grad, shift_grad = norm_backward(
            normed_grad, unit_norm, inv_std, gain_rows[0]
        )
        gain_all = jnp.concatenate([gain_grad[None], jnp.zeros((2, d_model), jnp.float32)], 0)
        bias_all = jnp.concatenate(
            [
                shift_grad[None],
                inner_bias_grad.reshape(hidden_width // d_model, d_model),
                outer_bias_grad[None],
            ],
            0,
        )
        table_all = jnp.stack([table_zero, table_zero])
        return (
            grad + stream_grad,
            token_zero,
            first_grad,
            second_grad,
            gain_all,
            bias_all,
            table_all,
        )

    def backward_shifted(saved, grad, blank_now):
        unit_norm, inv_std, normed_b, packed, wide_f, log_total = saved[:6]
        stream_grad, pieces = attention_backward(
            grad,
            (unit_norm, inv_std, normed_b, packed, log_total),
            first_rows,
            gain_rows[1 - 1],
            tables[1],
            blank_now,
            True,
            onehot,
        )
        (
            weight_grad,
            gain_grad,
            shift_grad,
            query_bias_grad,
            value_bias_grad,
            output_bias_grad,
            table_grad,
        ) = pieces
        second_grad = jnp.zeros((hidden_width, d_model), jnp.float32)
        gain_all = jnp.concatenate([gain_grad[None], jnp.zeros((2, d_model), jnp.float32)], 0)
        bias_all = jnp.concatenate(
            [
                jnp.stack([shift_grad, query_bias_grad, value_bias_grad, output_bias_grad]),
                jnp.zeros((2, d_model), jnp.float32),
            ],
            0,
        )
        table_all = jnp.stack([table_zero, table_grad])
        return (stream_grad, token_zero, weight_grad, second_grad, gain_all, bias_all, table_all)

    def run_forward(stream, tokens_now, blank_now):
        return lax.switch(
            section_index,
            [forward_first, forward_mlp, forward_shifted, forward_mlp],
            stream,
            tokens_now,
            blank_now,
        )

    def run_backward(saved, grad, blank_now):
        return lax.switch(
            section_index,
            [backward_first, backward_mlp, backward_shifted, backward_mlp],
            saved,
            grad,
            blank_now,
        )

    stored = jnp.zeros((micro_count, token_count, d_model), jnp.bfloat16)
    produced = jnp.zeros((micro_count, token_count, d_model), jnp.float32)

    def forward_tick(tick_index, carry):
        incoming, produced, stored = carry
        micro_index = tick_index - section_index
        is_valid = (micro_index >= 0) & (micro_index < micro_count)
        micro_slot = jnp.clip(micro_index, 0, micro_count - 1)
        result, saved = run_forward(
            incoming.astype(jnp.float32), page_tokens[micro_slot], blank[micro_slot]
        )
        sending = result.astype(jnp.bfloat16)
        is_last = is_valid & (section_index == sections - 1)
        produced = produced.at[micro_slot].set(
            jnp.where(is_last, sending.astype(jnp.float32), produced[micro_slot])
        )
        stored = stored.at[micro_slot].set(jnp.where(is_valid, incoming, stored[micro_slot]))
        incoming = shifted_2(sending, "pipe", 1)
        return (incoming, produced, stored)

    start_acts = jnp.zeros((token_count, d_model), jnp.bfloat16)
    incoming, produced, stored = lax.fori_loop(
        0, micro_count + sections - 1, forward_tick, (start_acts, produced, stored)
    )
    totals = (
        jnp.zeros((d_model, hidden_width), jnp.float32),
        jnp.zeros((hidden_width, d_model), jnp.float32),
        jnp.zeros(gain_rows.shape, jnp.float32),
        jnp.zeros(bias_rows.shape, jnp.float32),
    )
    table_total = jnp.zeros(tables.shape, jnp.float32)
    token_grads = jnp.zeros(page_tokens.shape, jnp.float32)

    def backward_tick(tick_index, carry):
        incoming, token_grads, totals, table_total = carry
        micro_index = tick_index - (sections - 1 - section_index)
        is_valid = (micro_index >= 0) & (micro_index < micro_count)
        micro_slot = jnp.clip(micro_index, 0, micro_count - 1)
        grad = jnp.where(
            section_index == sections - 1,
            cotangent[micro_slot].astype(jnp.float32),
            incoming.astype(jnp.float32),
        )
        saved = run_forward(
            stored[micro_slot].astype(jnp.float32), page_tokens[micro_slot], blank[micro_slot]
        )[1]
        stream_grad, token_grad, first_term, second_term, gain_term, bias_term, table_term = (
            run_backward(saved, grad, blank[micro_slot])
        )
        first_term = jnp.where(is_valid, first_term, 0.0)
        second_term = jnp.where(is_valid, second_term, 0.0)
        gain_term = jnp.where(is_valid, gain_term, 0.0)
        bias_term = jnp.where(is_valid, bias_term, 0.0)
        table_total = table_total + jnp.where(is_valid, table_term, 0.0)
        is_first = is_valid & (section_index == 0)
        token_grads = token_grads.at[micro_slot].set(
            jnp.where(is_first, token_grad, token_grads[micro_slot])
        )
        totals = (
            totals[0] + first_term,
            totals[1] + second_term,
            totals[2] + gain_term,
            totals[3] + bias_term,
        )
        incoming = shifted_2(stream_grad.astype(jnp.bfloat16), "pipe", -1)
        return (incoming, token_grads, totals, table_total)

    incoming, token_grads, totals, table_total = lax.fori_loop(
        0, micro_count + sections - 1, backward_tick, (start_acts, token_grads, totals, table_total)
    )
    shares = (
        lax.psum_scatter(totals[0], "wide", scatter_dimension=0, tiled=True),
        lax.psum_scatter(totals[1], "wide", scatter_dimension=1, tiled=True),
        lax.psum_scatter(totals[2], "wide", scatter_dimension=1, tiled=True),
        lax.psum_scatter(totals[3], "wide", scatter_dimension=1, tiled=True),
    )
    table_sum = lax.psum(table_total, ("pipe", "wide"))
    output_sum, input_sum = (
        lax.psum_scatter(
            produced.astype(jnp.bfloat16), "pipe", scatter_dimension=2, tiled=True
        ).astype(jnp.float32),
        lax.psum_scatter(
            token_grads.astype(jnp.bfloat16), "pipe", scatter_dimension=3, tiled=True
        ).astype(jnp.float32),
    )
    return (
        output_sum.astype(jnp.bfloat16),
        input_sum,
        shares[0][None],
        shares[1][None],
        shares[2][None],
        shares[3][None],
        table_sum,
    )


def solution(mesh):
    placed = (
        P("wide", None, None, None),
        P("wide", None),
        P("wide", None, None),
        P("pipe", None, None),
        P("pipe", None, None),
        P("pipe", None, None),
        P("pipe", None, None),
        P(),
    )
    return jax.shard_map(
        local,
        mesh=mesh,
        in_specs=placed,
        out_specs=(
            P("wide", None, "pipe"),
            P("wide", None, None, "pipe"),
            P("pipe", "wide", None),
            P("pipe", None, "wide"),
            P("pipe", None, "wide"),
            P("pipe", None, "wide"),
            P(),
        ),
        check_vma=False,
    )
```

profile of v0, /device:TPU:15, one launch (start us, length us, event | category | flops | bytes accessed | tf_op | source)
XLA Modules:
  0.0 3565.6 jit_solution(5021219039468454796)
XLA Ops:
  16.7 567.9 %while.54 = (s32[]{:T(128)}, bf16[200,1024]{1,0:T(8,128)(2,1)S(1)}, bf16[3,200,1024]{2,1,0:T(8,128)(2,1)}, bf16[3,200,1024]{2,1,0:T(8,128)(2,1)}, s32[]{:T(128)}...) while((s32[]{:T(128)}, bf16[200,1024]{1,0:T(8,128)(2,1)S(1)}, ...), condition=%wide.region_20.21_spmd.clone.clone, body=%wide.region_0.20_spmd.clone.clone.sunk | while | flops 4005074688 | bytes 146612352 | solution.py:534
  25.8 26.1 conditional.12
  57.9 51.4 %collective-permute-done = bf16[200,1024]{1,0:T(8,128)(2,1)S(1)} collective-permute-done((bf16[200,1024]{1,0:T(8,128)(2,1)}, bf16[200,1024]{1,0:T(8,128)(2,1)S(1)}, u32[]{:S(2)}, u32[]{:S(2)}) %collective-permute-start) | collective-permute-done | bytes 409632 | tf_op jit(solution)/shard_map/while/body/eval_jaxpr/ppermute | solution.py:19
  135.6 69.5 %collective-permute-done = bf16[200,1024]{1,0:T(8,128)(2,1)S(1)} collective-permute-done((bf16[200,1024]{1,0:T(8,128)(2,1)}, bf16[200,1024]{1,0:T(8,128)(2,1)S(1)}, u32[]{:S(2)}, u32[]{:S(2)}) %collective-permute-start) | collective-permute-done | bytes 409632 | tf_op jit(solution)/shard_map/while/body/eval_jaxpr/ppermute | solution.py:19
  231.1 63.8 %collective-permute-done = bf16[200,1024]{1,0:T(8,128)(2,1)S(1)} collective-permute-done((bf16[200,1024]{1,0:T(8,128)(2,1)}, bf16[200,1024]{1,0:T(8,128)(2,1)S(1)}, u32[]{:S(2)}, u32[]{:S(2)}) %collective-permute-start) | collective-permute-done | bytes 409632 | tf_op jit(solution)/shard_map/while/body/eval_jaxpr/ppermute | solution.py:19
  320.9 63.8 %collective-permute-done = bf16[200,1024]{1,0:T(8,128)(2,1)S(1)} collective-permute-done((bf16[200,1024]{1,0:T(8,128)(2,1)}, bf16[200,1024]{1,0:T(8,128)(2,1)S(1)}, u32[]{:S(2)}, u32[]{:S(2)}) %collective-permute-start) | collective-permute-done | bytes 409632 | tf_op jit(solution)/shard_map/while/body/eval_jaxpr/ppermute | solution.py:19
  410.7 63.8 %collective-permute-done = bf16[200,1024]{1,0:T(8,128)(2,1)S(1)} collective-permute-done((bf16[200,1024]{1,0:T(8,128)(2,1)}, bf16[200,1024]{1,0:T(8,128)(2,1)S(1)}, u32[]{:S(2)}, u32[]{:S(2)}) %collective-permute-start) | collective-permute-done | bytes 409632 | tf_op jit(solution)/shard_map/while/body/eval_jaxpr/ppermute | solution.py:19
  500.5 82.5 %collective-permute-done = bf16[200,1024]{1,0:T(8,128)(2,1)S(1)} collective-permute-done((bf16[200,1024]{1,0:T(8,128)(2,1)}, bf16[200,1024]{1,0:T(8,128)(2,1)S(1)}, u32[]{:S(2)}, u32[]{:S(2)}) %collective-permute-start) | collective-permute-done | bytes 409632 | tf_op jit(solution)/shard_map/while/body/eval_jaxpr/ppermute | solution.py:19
  586.3 1951.2 %while.55 = (s32[]{:T(128)}, bf16[200,1024]{1,0:T(8,128)(2,1)S(1)}, bf16[3,40,20,512]{3,1,2,0:T(8,128)(2,1)}, f32[1024,4096]{0,1:T(8,128)}, f32[4096,1024]{1,0:T...) while((s32[]{:T(128)}, bf16[200,1024]{1,0:T(8,128)(2,1)S(1)}, ...), condition=%wide.region_82.83_spmd.clone.clone, body=%wide.region_22.82_spmd.clone.clone.sunk | while | flops 11659542528 | bytes 669181952 | solution.py:580
  602.1 29.1 conditional.13
  631.2 60.6 %conditional.14 = (bf16[200,1024]{1,0:T(8,128)(2,1)}, bf16[40,20,512]{2,1,0:T(8,128)(2,1)S(1)}, f32[1024,4096]{0,1:T(8,128)}, f32[4096,1024]{1,0:T(8,128)}, f32[...) conditional(s32[]{:T(128)} %get-tuple-element.2891, ...), branch_computations={%region_41.54_spmd, %region_55.61_spmd, %region_62.73_spmd, %regio... | conditional | flops 8036967936 | bytes 278319040 | solution.py:505
  691.8 211.3 %collective-permute-start.1 = (bf16[200,1024]{1,0:T(8,128)(2,1)}, bf16[200,1024]{1,0:T(8,128)(2,1)S(1)}, u32[]{:S(2)}, u32[]{:S(2)}) collective-permute-start(bf16[200,1024]{1,0:T(8,128)(2,1)} %get-tuple-element.2640), channel_id=1, source_target_pairs={{8,0},{16,8},{24,16},{9,1},{17,9},{25,17},{10,2},{18,10},{26,18},{... | collective-permute-start | bytes 1228808 | tf_op jit(solution)/shard_map/while/body/eval_jaxpr/ppermute | solution.py:19
  947.7 29.1 conditional.13
  976.8 60.6 %conditional.14 = (bf16[200,1024]{1,0:T(8,128)(2,1)}, bf16[40,20,512]{2,1,0:T(8,128)(2,1)S(1)}, f32[1024,4096]{0,1:T(8,128)}, f32[4096,1024]{1,0:T(8,128)}, f32[...) conditional(s32[]{:T(128)} %get-tuple-element.2891, ...), branch_computations={%region_41.54_spmd, %region_55.61_spmd, %region_62.73_spmd, %regio... | conditional | flops 8036967936 | bytes 278319040 | solution.py:505
  1037.4 172.8 %collective-permute-start.1 = (bf16[200,1024]{1,0:T(8,128)(2,1)}, bf16[200,1024]{1,0:T(8,128)(2,1)S(1)}, u32[]{:S(2)}, u32[]{:S(2)}) collective-permute-start(bf16[200,1024]{1,0:T(8,128)(2,1)} %get-tuple-element.2640), channel_id=1, source_target_pairs={{8,0},{16,8},{24,16},{9,1},{17,9},{25,17},{10,2},{18,10},{26,18},{... | collective-permute-start | bytes 1228808 | tf_op jit(solution)/shard_map/while/body/eval_jaxpr/ppermute | solution.py:19
  1259.6 29.1 conditional.13
  1288.8 60.6 %conditional.14 = (bf16[200,1024]{1,0:T(8,128)(2,1)}, bf16[40,20,512]{2,1,0:T(8,128)(2,1)S(1)}, f32[1024,4096]{0,1:T(8,128)}, f32[4096,1024]{1,0:T(8,128)}, f32[...) conditional(s32[]{:T(128)} %get-tuple-element.2891, ...), branch_computations={%region_41.54_spmd, %region_55.61_spmd, %region_62.73_spmd, %regio... | conditional | flops 8036967936 | bytes 278319040 | solution.py:505
  1349.4 181.0 %collective-permute-start.1 = (bf16[200,1024]{1,0:T(8,128)(2,1)}, bf16[200,1024]{1,0:T(8,128)(2,1)S(1)}, u32[]{:S(2)}, u32[]{:S(2)}) collective-permute-start(bf16[200,1024]{1,0:T(8,128)(2,1)} %get-tuple-element.2640), channel_id=1, source_target_pairs={{8,0},{16,8},{24,16},{9,1},{17,9},{25,17},{10,2},{18,10},{26,18},{... | collective-permute-start | bytes 1228808 | tf_op jit(solution)/shard_map/while/body/eval_jaxpr/ppermute | solution.py:19
  1579.9 29.1 conditional.13
  1609.0 60.6 %conditional.14 = (bf16[200,1024]{1,0:T(8,128)(2,1)}, bf16[40,20,512]{2,1,0:T(8,128)(2,1)S(1)}, f32[1024,4096]{0,1:T(8,128)}, f32[4096,1024]{1,0:T(8,128)}, f32[...) conditional(s32[]{:T(128)} %get-tuple-element.2891, ...), branch_computations={%region_41.54_spmd, %region_55.61_spmd, %region_62.73_spmd, %regio... | conditional | flops 8036967936 | bytes 278319040 | solution.py:505
  1669.6 181.0 %collective-permute-start.1 = (bf16[200,1024]{1,0:T(8,128)(2,1)}, bf16[200,1024]{1,0:T(8,128)(2,1)S(1)}, u32[]{:S(2)}, u32[]{:S(2)}) collective-permute-start(bf16[200,1024]{1,0:T(8,128)(2,1)} %get-tuple-element.2640), channel_id=1, source_target_pairs={{8,0},{16,8},{24,16},{9,1},{17,9},{25,17},{10,2},{18,10},{26,18},{... | collective-permute-start | bytes 1228808 | tf_op jit(solution)/shard_map/while/body/eval_jaxpr/ppermute | solution.py:19
  1891.8 29.1 conditional.13
  1920.9 60.6 %conditional.14 = (bf16[200,1024]{1,0:T(8,128)(2,1)}, bf16[40,20,512]{2,1,0:T(8,128)(2,1)S(1)}, f32[1024,4096]{0,1:T(8,128)}, f32[4096,1024]{1,0:T(8,128)}, f32[...) conditional(s32[]{:T(128)} %get-tuple-element.2891, ...), branch_computations={%region_41.54_spmd, %region_55.61_spmd, %region_62.73_spmd, %regio... | conditional | flops 8036967936 | bytes 278319040 | solution.py:505
  1981.6 189.3 %collective-permute-start.1 = (bf16[200,1024]{1,0:T(8,128)(2,1)}, bf16[200,1024]{1,0:T(8,128)(2,1)S(1)}, u32[]{:S(2)}, u32[]{:S(2)}) collective-permute-start(bf16[200,1024]{1,0:T(8,128)(2,1)} %get-tuple-element.2640), channel_id=1, source_target_pairs={{8,0},{16,8},{24,16},{9,1},{17,9},{25,17},{10,2},{18,10},{26,18},{... | collective-permute-start | bytes 1228808 | tf_op jit(solution)/shard_map/while/body/eval_jaxpr/ppermute | solution.py:19
  2212.0 29.1 conditional.13
  2241.2 60.6 %conditional.14 = (bf16[200,1024]{1,0:T(8,128)(2,1)}, bf16[40,20,512]{2,1,0:T(8,128)(2,1)S(1)}, f32[1024,4096]{0,1:T(8,128)}, f32[4096,1024]{1,0:T(8,128)}, f32[...) conditional(s32[]{:T(128)} %get-tuple-element.2891, ...), branch_computations={%region_41.54_spmd, %region_55.61_spmd, %region_62.73_spmd, %regio... | conditional | flops 8036967936 | bytes 278319040 | solution.py:505
  2301.8 202.2 %collective-permute-start.1 = (bf16[200,1024]{1,0:T(8,128)(2,1)}, bf16[200,1024]{1,0:T(8,128)(2,1)S(1)}, u32[]{:S(2)}, u32[]{:S(2)}) collective-permute-start(bf16[200,1024]{1,0:T(8,128)(2,1)} %get-tuple-element.2640), channel_id=1, source_target_pairs={{8,0},{16,8},{24,16},{9,1},{17,9},{25,17},{10,2},{18,10},{26,18},{... | collective-permute-start | bytes 1228808 | tf_op jit(solution)/shard_map/while/body/eval_jaxpr/ppermute | solution.py:19
  2581.4 280.4 %reduce-scatter.21.cloned.1.call-done = f32[128,3]{1,0:T(8,128)} async-done(((f32[1024,3]{1,0:T(8,128)}), f32[128,3]{1,0:T(8,128)}) %reduce-scatter.21.cloned.1.call-update) | async-done | bytes 1552
  2863.3 54.3 %reduce-scatter.17.cloned.1.call-done = f32[6,128]{1,0:T(8,128)} async-done(((f32[6,1024]{1,0:T(8,128)}), f32[6,128]{1,0:T(8,128)}) %reduce-scatter.17.cloned.1.call-update) | async-done | bytes 3088 | tf_op jit(solution)/shard_map/reduce_scatter | solution.py:587
  2918.9 35.8 %reduce-scatter.19.cloned.1.call-done = bf16[128,2400]{1,0:T(8,128)(2,1)} async-done(((bf16[512,2400]{1,0:T(8,128)(2,1)}), bf16[128,2400]{1,0:T(8,128)(2,1)}) %reduce-scatter.19.cloned.1.call-update) | async-done | bytes 614416
  2983.8 286.6 %reduce-scatter.13.cloned.1.call-done = f32[128,4096]{1,0:T(8,128)} async-done(((f32[1024,4096]{1,0:T(8,128)}), f32[128,4096]{1,0:T(8,128)}) %reduce-scatter.13.cloned.1.call-update) | async-done | bytes 2097168 | tf_op jit(solution)/shard_map/reduce_scatter | solution.py:584
  3270.3 286.1 %reduce-scatter.15.cloned.1.call-done = f32[4096,128]{1,0:T(8,128)} async-done(((f32[4096,1024]{1,0:T(8,128)}), f32[4096,128]{1,0:T(8,128)}) %reduce-scatter.15.cloned.1.call-update) | async-done | bytes 2097168 | tf_op jit(solution)/shard_map/reduce_scatter | solution.py:585
  (598 shorter events, 821.4 us)
Async XLA Ops:
  8.0 2853.8 %reduce-scatter.21.cloned.1.call-start = ((), (), s32[]{:S(2)}) async-start(), calls=%async_computation.12 | async-start | bytes 589824
  51.9 57.3 %collective-permute-start = (bf16[200,1024]{1,0:T(8,128)(2,1)}, bf16[200,1024]{1,0:T(8,128)(2,1)S(1)}, u32[]{:S(2)}, u32[]{:S(2)}) collective-permute-start(bf16[200,1024]{1,0:T(8,128)(2,1)} %get-tuple-element.2600), channel_id=1, source_target_pairs={{0,8},{8,16},{16,24},{1,9},{9,17},{17,25},{2,10},{10,18},{18,26},{... | collective-permute-start | bytes 1228808 | tf_op jit(solution)/shard_map/while/body/eval_jaxpr/ppermute | solution.py:19
  129.7 75.4 %collective-permute-start = (bf16[200,1024]{1,0:T(8,128)(2,1)}, bf16[200,1024]{1,0:T(8,128)(2,1)S(1)}, u32[]{:S(2)}, u32[]{:S(2)}) collective-permute-start(bf16[200,1024]{1,0:T(8,128)(2,1)} %get-tuple-element.2600), channel_id=1, source_target_pairs={{0,8},{8,16},{16,24},{1,9},{9,17},{17,25},{2,10},{10,18},{18,26},{... | collective-permute-start | bytes 1228808 | tf_op jit(solution)/shard_map/while/body/eval_jaxpr/ppermute | solution.py:19
  225.2 69.7 %collective-permute-start = (bf16[200,1024]{1,0:T(8,128)(2,1)}, bf16[200,1024]{1,0:T(8,128)(2,1)S(1)}, u32[]{:S(2)}, u32[]{:S(2)}) collective-permute-start(bf16[200,1024]{1,0:T(8,128)(2,1)} %get-tuple-element.2600), channel_id=1, source_target_pairs={{0,8},{8,16},{16,24},{1,9},{9,17},{17,25},{2,10},{10,18},{18,26},{... | collective-permute-start | bytes 1228808 | tf_op jit(solution)/shard_map/while/body/eval_jaxpr/ppermute | solution.py:19
  315.0 69.7 %collective-permute-start = (bf16[200,1024]{1,0:T(8,128)(2,1)}, bf16[200,1024]{1,0:T(8,128)(2,1)S(1)}, u32[]{:S(2)}, u32[]{:S(2)}) collective-permute-start(bf16[200,1024]{1,0:T(8,128)(2,1)} %get-tuple-element.2600), channel_id=1, source_target_pairs={{0,8},{8,16},{16,24},{1,9},{9,17},{17,25},{2,10},{10,18},{18,26},{... | collective-permute-start | bytes 1228808 | tf_op jit(solution)/shard_map/while/body/eval_jaxpr/ppermute | solution.py:19
  404.8 69.7 %collective-permute-start = (bf16[200,1024]{1,0:T(8,128)(2,1)}, bf16[200,1024]{1,0:T(8,128)(2,1)S(1)}, u32[]{:S(2)}, u32[]{:S(2)}) collective-permute-start(bf16[200,1024]{1,0:T(8,128)(2,1)} %get-tuple-element.2600), channel_id=1, source_target_pairs={{0,8},{8,16},{16,24},{1,9},{9,17},{17,25},{2,10},{10,18},{18,26},{... | collective-permute-start | bytes 1228808 | tf_op jit(solution)/shard_map/while/body/eval_jaxpr/ppermute | solution.py:19
  494.6 88.4 %collective-permute-start = (bf16[200,1024]{1,0:T(8,128)(2,1)}, bf16[200,1024]{1,0:T(8,128)(2,1)S(1)}, u32[]{:S(2)}, u32[]{:S(2)}) collective-permute-start(bf16[200,1024]{1,0:T(8,128)(2,1)} %get-tuple-element.2600), channel_id=1, source_target_pairs={{0,8},{8,16},{16,24},{1,9},{9,17},{17,25},{2,10},{10,18},{18,26},{... | collective-permute-start | bytes 1228808 | tf_op jit(solution)/shard_map/while/body/eval_jaxpr/ppermute | solution.py:19
  691.8 211.4 %copy-start.43 = (f32[2,32,361]{2,1,0:T(8,128)}, f32[2,32,361]{2,1,0:T(8,128)S(1)}, u32[]{:S(2)}) copy-start(f32[2,32,361]{2,1,0:T(8,128)S(1)} %get-tuple-element.2646) | copy-start | bytes 277252 | tf_op jit(solution)/shard_map/while
  691.8 241.7 %collective-permute-start.1 = (bf16[200,1024]{1,0:T(8,128)(2,1)}, bf16[200,1024]{1,0:T(8,128)(2,1)S(1)}, u32[]{:S(2)}, u32[]{:S(2)}) collective-permute-start(bf16[200,1024]{1,0:T(8,128)(2,1)} %get-tuple-element.2640), channel_id=1, source_target_pairs={{8,0},{16,8},{24,16},{9,1},{17,9},{25,17},{10,2},{18,10},{26,18},{... | collective-permute-start | bytes 1228808 | tf_op jit(solution)/shard_map/while/body/eval_jaxpr/ppermute | solution.py:19
  1037.4 172.8 %copy-start.43 = (f32[2,32,361]{2,1,0:T(8,128)}, f32[2,32,361]{2,1,0:T(8,128)S(1)}, u32[]{:S(2)}) copy-start(f32[2,32,361]{2,1,0:T(8,128)S(1)} %get-tuple-element.2646) | copy-start | bytes 277252 | tf_op jit(solution)/shard_map/while
  1037.4 208.0 %collective-permute-start.1 = (bf16[200,1024]{1,0:T(8,128)(2,1)}, bf16[200,1024]{1,0:T(8,128)(2,1)S(1)}, u32[]{:S(2)}, u32[]{:S(2)}) collective-permute-start(bf16[200,1024]{1,0:T(8,128)(2,1)} %get-tuple-element.2640), channel_id=1, source_target_pairs={{8,0},{16,8},{24,16},{9,1},{17,9},{25,17},{10,2},{18,10},{26,18},{... | collective-permute-start | bytes 1228808 | tf_op jit(solution)/shard_map/while/body/eval_jaxpr/ppermute | solution.py:19
  1211.5 18.4 slice-start
  1211.5 18.5 slice-start.1
  1211.5 20.3 slice-start.2
  1211.5 21.5 slice-start.3
  1349.4 181.1 %copy-start.43 = (f32[2,32,361]{2,1,0:T(8,128)}, f32[2,32,361]{2,1,0:T(8,128)S(1)}, u32[]{:S(2)}) copy-start(f32[2,32,361]{2,1,0:T(8,128)S(1)} %get-tuple-element.2646) | copy-start | bytes 277252 | tf_op jit(solution)/shard_map/while
  1349.4 216.3 %collective-permute-start.1 = (bf16[200,1024]{1,0:T(8,128)(2,1)}, bf16[200,1024]{1,0:T(8,128)(2,1)S(1)}, u32[]{:S(2)}, u32[]{:S(2)}) collective-permute-start(bf16[200,1024]{1,0:T(8,128)(2,1)} %get-tuple-element.2640), channel_id=1, source_target_pairs={{8,0},{16,8},{24,16},{9,1},{17,9},{25,17},{10,2},{18,10},{26,18},{... | collective-permute-start | bytes 1228808 | tf_op jit(solution)/shard_map/while/body/eval_jaxpr/ppermute | solution.py:19
  1531.7 18.5 slice-start.1
  1531.7 20.3 slice-start.2
  1531.7 21.5 slice-start.3
  1669.6 181.1 %copy-start.43 = (f32[2,32,361]{2,1,0:T(8,128)}, f32[2,32,361]{2,1,0:T(8,128)S(1)}, u32[]{:S(2)}) copy-start(f32[2,32,361]{2,1,0:T(8,128)S(1)} %get-tuple-element.2646) | copy-start | bytes 277252 | tf_op jit(solution)/shard_map/while
  1669.6 208.1 %collective-permute-start.1 = (bf16[200,1024]{1,0:T(8,128)(2,1)}, bf16[200,1024]{1,0:T(8,128)(2,1)S(1)}, u32[]{:S(2)}, u32[]{:S(2)}) collective-permute-start(bf16[200,1024]{1,0:T(8,128)(2,1)} %get-tuple-element.2640), channel_id=1, source_target_pairs={{8,0},{16,8},{24,16},{9,1},{17,9},{25,17},{10,2},{18,10},{26,18},{... | collective-permute-start | bytes 1228808 | tf_op jit(solution)/shard_map/while/body/eval_jaxpr/ppermute | solution.py:19
  1981.6 189.3 %copy-start.43 = (f32[2,32,361]{2,1,0:T(8,128)}, f32[2,32,361]{2,1,0:T(8,128)S(1)}, u32[]{:S(2)}) copy-start(f32[2,32,361]{2,1,0:T(8,128)S(1)} %get-tuple-element.2646) | copy-start | bytes 277252 | tf_op jit(solution)/shard_map/while
  1981.6 216.3 %collective-permute-start.1 = (bf16[200,1024]{1,0:T(8,128)(2,1)}, bf16[200,1024]{1,0:T(8,128)(2,1)S(1)}, u32[]{:S(2)}, u32[]{:S(2)}) collective-permute-start(bf16[200,1024]{1,0:T(8,128)(2,1)} %get-tuple-element.2640), channel_id=1, source_target_pairs={{8,0},{16,8},{24,16},{9,1},{17,9},{25,17},{10,2},{18,10},{26,18},{... | collective-permute-start | bytes 1228808 | tf_op jit(solution)/shard_map/while/body/eval_jaxpr/ppermute | solution.py:19
  2301.8 202.2 %copy-start.43 = (f32[2,32,361]{2,1,0:T(8,128)}, f32[2,32,361]{2,1,0:T(8,128)S(1)}, u32[]{:S(2)}) copy-start(f32[2,32,361]{2,1,0:T(8,128)S(1)} %get-tuple-element.2646) | copy-start | bytes 277252 | tf_op jit(solution)/shard_map/while
  2301.8 229.2 %collective-permute-start.1 = (bf16[200,1024]{1,0:T(8,128)(2,1)}, bf16[200,1024]{1,0:T(8,128)(2,1)S(1)}, u32[]{:S(2)}, u32[]{:S(2)}) collective-permute-start(bf16[200,1024]{1,0:T(8,128)(2,1)} %get-tuple-element.2640), channel_id=1, source_target_pairs={{8,0},{16,8},{24,16},{9,1},{17,9},{25,17},{10,2},{18,10},{26,18},{... | collective-permute-start | bytes 1228808 | tf_op jit(solution)/shard_map/while/body/eval_jaxpr/ppermute | solution.py:19
  2539.3 378.3 %reduce-scatter.17.cloned.1.call-start = ((), (), s32[]{:S(2)}) async-start(), calls=%async_computation.9 | async-start | bytes 36864 | tf_op jit(solution)/shard_map/reduce_scatter | solution.py:587
  2540.1 414.6 %reduce-scatter.19.cloned.1.call-start = ((), (), s32[]{:S(2)}) async-start(), calls=%async_computation.11 | async-start | bytes 3112960
  2562.1 398.8 %all-reduce.8.cloned.1.call-start = ((), (), s32[]{:S(2)}) async-start(), calls=%async_computation.10 | async-start | bytes 196608 | tf_op jit(solution)/shard_map/psum | solution.py:589
  2562.7 421.1 %reduce-scatter.11.cloned.1.call-start = ((), (), s32[]{:S(2)}) async-start(), calls=%async_computation.6 | async-start | bytes 1536000 | tf_op jit(solution)/shard_map/reduce_scatter | solution.py:591
  2563.3 707.0 %reduce-scatter.13.cloned.1.call-start = ((), (), s32[]{:S(2)}) async-start(), calls=%async_computation.7 | async-start | bytes 18874368 | tf_op jit(solution)/shard_map/reduce_scatter | solution.py:584
  2580.8 975.6 %reduce-scatter.15.cloned.1.call-start = ((), (), s32[]{:S(2)}) async-start(), calls=%async_computation.8 | async-start | bytes 18874368 | tf_op jit(solution)/shard_map/reduce_scatter | solution.py:585
  (96 other events, 837.2 us)
Sparse Core Ops, SparseCore 0:
  2539.4 322.3 reduce-scatter.20
  2865.3 52.3 reduce-scatter.16
  2920.4 34.2 reduce-scatter.18
  2957.7 26.0 reduce-scatter.10
  2988.5 281.8 reduce-scatter.12
  3274.6 281.8 reduce-scatter.14
Sparse Core Ops, SparseCore 1:
  2569.7 389.4 all-reduce.7
where the time goes:
time: 3590 us; the launch traced here: 3570 us
  waiting for transfers between devices  1360 us (38%)
  starting transfers between devices  1150 us (32%)
  loops' own time  308 us (9%)
  other arithmetic  307 us (9%)
  matrix products  259 us (7%)
  local copies, waits for them, and re-layouts  167 us (5%)
    ppermute x12, starting transfers between devices, shifted_2(): return lax.ppermute(array, axis, pairs)  1150 us
    ppermute x12, waiting for transfers between devices, shifted_2(): return lax.ppermute(array, axis, pairs)  395 us
    unnamed x9, waiting for transfers between devices  319 us
    reduce_scatter x1, waiting for transfers between devices, local(): lax.psum_scatter(totals[0], 'wide', scatter_dimension=0, tiled=True)  287 us
    reduce_scatter x1, waiting for transfers between devices, local(): lax.psum_scatter(totals[1], 'wide', scatter_dimension=1, tiled=True)  286 us
    another operation x6, loops' own time, run_backward(): lax.switch(section_index, [backward_first, backward_mlp, backward_shifted...  184 us
    another operation x12, loops' own time, run_forward(): lax.switch(section_index, [forward_first, forward_mlp, forward_shifted, f...  110 us
    dot_general x12, matrix products, outer_sum(): lax.dot_general(left, right, (((0,), (0,)), ((), ())), preferred_element_...  104 us
  transfers between devices with their start and end apart: 19, of which 12 were waited for; matrix products, arithmetic and copies ran while one was open for 7% of the time, Pallas kernels for 0%

commit v1 on v0

v1 whole, which is shorter than its diff:
```python
import functools
from itertools import zip_longest

import jax
import jax.numpy as jnp
import numpy as np
from jax import lax
from jax.experimental import pallas as pl
from jax.experimental.pallas import tpu as pltpu
from jax.sharding import PartitionSpec as P

HEADS = 32
WIN = 10
GRID_H = 20
GRID_W = 10
AREA = WIN * WIN
TOK = GRID_H * GRID_W
ROWS = 112
WINS = 3
M = ROWS * WINS
D = 1024
FF = 4096
CHUNK = 512
EPSILON = 1e-05
NEGATIVE = -1000000000.0
SCALE = 32 ** (-0.5)
MESH = pl.DeviceIdType.MESH
F32 = jnp.float32
BF16 = jnp.bfloat16


def shape_of(dims, kind):
    return jax.ShapeDtypeStruct(dims, kind)


def dot(left, right):
    return jnp.dot(left, right, preferred_element_type=F32)


def dot_nt(left, right):
    return lax.dot_general(left, right, (((1,), (1,)), ((), ())), preferred_element_type=F32)


def dot_tn(left, right):
    return lax.dot_general(left, right, (((0,), (0,)), ((), ())), preferred_element_type=F32)


def norm_parts(values):
    average = jnp.mean(values, -1, keepdims=True)
    centered = values - average
    inv_std = lax.rsqrt(jnp.mean(centered * centered, -1, keepdims=True) + EPSILON)
    return centered * inv_std, inv_std


def norm_backward(grad_out, values, gain):
    unit, inv_std = norm_parts(values)
    scaled = grad_out * gain
    grad_in = inv_std * (
        scaled
        - jnp.mean(scaled, -1, keepdims=True)
        - unit * jnp.mean(scaled * unit, -1, keepdims=True)
    )
    return (
        grad_in,
        jnp.sum(grad_out * unit, 0, keepdims=True),
        jnp.sum(grad_out, 0, keepdims=True),
    )


def split_dot(left, right, product=dot):
    high = left.astype(BF16)
    low = (left - high.astype(F32)).astype(BF16)
    return product(high, right) + product(low, right)


ANYWHERE = pl.BlockSpec(memory_space=pl.ANY)
IN_VMEM = pl.BlockSpec(memory_space=pltpu.VMEM)
DMA = pltpu.SemaphoreType.DMA
SPAN = 2 * WIN - 1
INNER = 256
OFFSETS = 384
GROUP = 256
GROUP_HEADS = GROUP // 32
STEPS = D // GROUP
CHUNKS = FF // CHUNK
PIECE = 256
HALF = FF // PIECE
PER = D // PIECE
RELAY = 12


class Refs:
    def __init__(self, names, refs):
        self.__dict__.update(zip(names, refs))


def lanes_at(start, size):
    return pl.ds(pl.multiple_of(start, 128), size)


def lane_masks():
    lanes = lax.broadcasted_iota(jnp.int32, (1, 128), 1)
    return [
        jnp.where((lanes >= 32 * h) & (lanes < 32 * h + 32), 1.0, 0.0).astype(BF16)
        for h in range(4)
    ]


def stacked(values, masks, rows):
    if rows > values.shape[0]:
        values = jnp.concatenate(
            [values, jnp.zeros((rows - values.shape[0], values.shape[1]), values.dtype)], 0
        )
    return jnp.concatenate([values * mask for mask in masks], 0)


def beside_ones(values, masks):
    ones = jnp.concatenate([jnp.broadcast_to(mask, (128, 128)) for mask in masks], 0)
    return jnp.concatenate([stacked(values, masks, 128), ones], 1)


def attention_forward(s, vec, weights):
    unit, _ = norm_parts(s.x[...])
    s.normed[...] = (unit * vec[0:1] + vec[3:4]).astype(BF16)
    s.acc[...] = jnp.zeros_like(s.acc)
    masks = lane_masks()

    def step(g, carry):
        weights(g)
        here = lanes_at(g * GROUP, GROUP)
        projected = dot(s.normed[...], s.w_qkv[g])
        s.qkv[0, :, here] = (projected[:, :GROUP] + vec[4:5, here]).astype(BF16)
        s.qkv[1, :, here] = projected[:, GROUP : 2 * GROUP].astype(BF16)
        s.qkv[2, :, here] = (projected[:, 2 * GROUP :] + vec[5:6, here]).astype(BF16)
        for w in range(WINS):
            rows = slice(w * ROWS, (w + 1) * ROWS)
            allowed = s.mask[w] > 0.5
            for part in range(GROUP // 128):
                lanes = lanes_at(g * GROUP + part * 128, 128)
                scores = dot_nt(s.qkv[0, rows, lanes], stacked(s.qkv[1, rows, lanes], masks, 128))
                found = []
                for h in range(4):
                    head = g * GROUP_HEADS + part * 4 + h
                    bias = s.rel[pl.ds(pl.multiple_of(head * ROWS, 8), ROWS)]
                    one = jnp.where(
                        allowed, scores[:, h * 128 : (h + 1) * 128] * SCALE + bias, NEGATIVE
                    )
                    exponent = jnp.exp(one - jnp.max(one, -1, keepdims=True)).astype(BF16)
                    s.exps[w, head] = exponent
                    found.append(exponent)
                sums = dot(jnp.concatenate(found, 1), beside_ones(s.qkv[2, rows, lanes], masks))
                scale = 1.0 / sums[:, 128:]
                s.inverse[rows, lanes] = scale
                s.mixed[rows, lanes] = (sums[:, :128] * scale).astype(BF16)
        s.acc[...] += dot(s.mixed[:, here], s.w_out[g])
        return carry

    lax.fori_loop(0, STEPS, step, 0)
    return s.x[...] + (s.acc[...] + vec[6:7])


def attention_backward(s, vec, right, vecs):
    masks = lane_masks()
    s.acc[...] = jnp.zeros_like(s.acc)

    def step(g, carry):
        here = lanes_at(g * GROUP, GROUP)
        mixed_grad = dot_nt(s.grad_a[...], s.w_out[g])
        scaled_grad = (mixed_grad * s.inverse[:, here]).astype(BF16)
        spread = (scaled_grad.astype(F32) * s.mixed[:, here].astype(F32)).astype(BF16)
        for w in range(WINS):
            rows = slice(w * ROWS, (w + 1) * ROWS)
            for part in range(GROUP // 128):
                inside = slice(part * 128, (part + 1) * 128)
                lanes = lanes_at(g * GROUP + part * 128, 128)
                grad_here = scaled_grad[rows, inside]
                prob_grad = dot_nt(
                    jnp.concatenate([grad_here, -spread[rows, inside]], 1),
                    beside_ones(s.qkv[2, rows, lanes], masks),
                )
                found = []
                draws = []
                for h in range(4):
                    head = g * GROUP_HEADS + part * 4 + h
                    exponent = s.exps[w, head]
                    score_grad = exponent.astype(F32) * prob_grad[:, h * 128 : (h + 1) * 128]
                    at = pl.ds(pl.multiple_of(head * ROWS, 8), ROWS)
                    if w == 0:
                        s.rel[at] = score_grad
                    else:
                        s.rel[at] += score_grad
                    found.append(exponent)
                    draws.append((score_grad * SCALE).astype(BF16))
                query_grad = dot(jnp.concatenate(draws, 1), stacked(s.qkv[1, rows, lanes], masks, 128))
                key_grad = dot_tn(jnp.concatenate(draws, 0), stacked(s.qkv[0, rows, lanes], masks, ROWS))
                value_grad = dot_tn(jnp.concatenate(found, 0), stacked(grad_here, masks, ROWS))
                right[0, rows, lanes] = query_grad.astype(BF16)
                right[1, rows, lanes] = key_grad[:ROWS].astype(BF16)
                right[2, rows, lanes] = value_grad[:ROWS].astype(BF16)
        joined = jnp.concatenate([right[k, :, here] for k in range(3)], 1)
        s.acc[...] += dot_nt(joined, s.w_qkv[g])
        return carry

    lax.fori_loop(0, STEPS, step, 0)
    grad_in, gain_grad, shift_grad = norm_backward(s.acc[...], s.x[...], vec[0:1])
    wide = s.grad_a[...].astype(F32)
    vecs[0:1] = gain_grad
    vecs[1:3] = jnp.zeros((2, D), F32)
    vecs[3:4] = shift_grad
    vecs[4:5] = jnp.sum(right[0].astype(F32), 0, keepdims=True)
    vecs[5:6] = jnp.sum(right[2].astype(F32), 0, keepdims=True)
    vecs[6:7] = jnp.sum(wide, 0, keepdims=True)
    vecs[7:16] = jnp.zeros((9, D), F32)
    return wide + grad_in


def gelu_parts(pre):
    cumulative = 0.5 * (1.0 + lax.erf(pre * 0.7071067811865476))
    density = jnp.exp(-0.5 * pre * pre) * 0.3989422804014327
    return (pre * cumulative).astype(BF16), (cumulative + pre * density).astype(BF16)


def mlp_forward(s, vec, weights):
    x = s.mid[...].astype(F32)
    unit, _ = norm_parts(x)
    s.normed[...] = (unit * vec[0:1] + vec[3:4]).astype(BF16)

    def product(j):
        weights(j)
        start = j % 2 * CHUNK
        bias = vec[4 + j // 2 : 5 + j // 2, start : start + CHUNK]
        s.pre[j % 2] = dot(s.normed[...], s.w1[j]) + bias

    def take(j):
        start = j % 2 * CHUNK
        term = dot(s.hidden[j // 2, :, start : start + CHUNK], s.w2[j])
        if j == 0:
            s.acc[...] = term
        else:
            s.acc[...] += term

    product(0)
    for j in range(CHUNKS):
        start = j % 2 * CHUNK
        if j + 1 < CHUNKS:
            product(j + 1)
        if j > 0:
            take(j - 1)
        values, slopes = gelu_parts(s.pre[j % 2])
        s.hidden[j // 2, :, start : start + CHUNK] = values
        s.slope[j // 2, :, start : start + CHUNK] = slopes
    take(CHUNKS - 1)
    return s.mid[...].astype(F32) + s.acc[...] + vec[8:9]


def mlp_backward(s, vec, vecs):
    def product(j):
        here = slice(j % 2 * CHUNK, (j % 2 + 1) * CHUNK)
        pre_grad = dot_nt(s.grad_m[...], s.w2[j]) * s.slope[j // 2, :, here].astype(F32)
        vecs[4 + j // 2 : 5 + j // 2, here] = jnp.sum(pre_grad, 0, keepdims=True)
        s.slope[j // 2, :, here] = pre_grad.astype(BF16)

    def take(j):
        here = slice(j % 2 * CHUNK, (j % 2 + 1) * CHUNK)
        term = dot_nt(s.slope[j // 2, :, here], s.w1[j])
        if j == 0:
            s.acc[...] = term
        else:
            s.acc[...] += term

    product(0)
    for j in range(CHUNKS):
        if j + 1 < CHUNKS:
            product(j + 1)
        take(j)
    grad_in, gain_grad, shift_grad = norm_backward(s.acc[...], s.mid[...].astype(F32), vec[0:1])
    wide = s.grad_m[...].astype(F32)
    vecs[0:1] = gain_grad
    vecs[1:3] = jnp.zeros((2, D), F32)
    vecs[3:4] = shift_grad
    vecs[8:9] = jnp.sum(wide, 0, keepdims=True)
    vecs[9:16] = jnp.zeros((7, D), F32)
    return wide + grad_in


def main_kernel(ins, outs, scratch, *refs):
    first = len(ins)
    second = first + len(outs)
    i, o, s = Refs(ins, refs[:first]), Refs(outs, refs[first:second]), Refs(scratch, refs[second:])
    p = lax.axis_index("pipe")
    w_at = lax.axis_index("wide")
    side, c = p // 2, lax.rem(p, 2)
    lower, upper = side == 0, side == 1
    pair = (p + 1 - 2 * c, w_at)
    across = (lax.rem(p + 2, 4), w_at)

    def local(source, target, sem):
        return pltpu.make_async_copy(source, target, sem)

    def remote(source, target, sent, got, to):
        return pltpu.make_async_remote_copy(
            source, target, sent, got, device_id=to, device_id_type=MESH
        )

    consts = [local(i.pack.at[k], s.hidden.at[k, :INNER], s.const_sem.at[k]) for k in range(4)]
    consts.append(local(i.pack.at[4], s.slope.at[0, :INNER], s.const_sem.at[4]))
    consts.append(local(i.roll.at[side, c], s.roll, s.const_sem.at[5]))
    picks = []
    for half in range(2):
        for source, target in (
            (i.pick.at[half, : 3 * ROWS], s.slope.at[1 + half]),
            (i.pick.at[half, 3 * ROWS :], s.slope.at[3, half * ROWS : (half + 1) * ROWS]),
        ):
            picks.append(local(source, target, s.pick_sem.at[len(picks)]))
    cot = local(i.cot.at[c], s.mixed, s.const_sem.at[6])

    def token_copy(k):
        return local(i.tokens.at[(c * WINS + k) // 2], s.tokens.at[k % 2], s.token_sem.at[k % 2])

    def cotangent_copy(k):
        return local(i.cotangent.at[k], s.cotangent, s.token_sem.at[0])

    for copy in consts:
        copy.start()

    @pl.when(lower)
    def _():
        token_copy(0).start()
        token_copy(1).start()
        for copy in picks:
            copy.start()

    @pl.when(upper)
    def _():
        cotangent_copy(0).start()
        cot.start()

    for row in range(3):
        s.vec[c, row : row + 1] = i.gains[row]
    for row in range(6):
        s.vec[c, 3 + row : 4 + row] = i.biases[row]
    s.vec[c, 9:16] = jnp.zeros((7, D), F32)
    barrier = pltpu.get_barrier_semaphore()
    for step in range(1, 4):
        pl.semaphore_signal(
            barrier, inc=1, device_id=(lax.rem(p + step, 4), w_at), device_id_type=MESH
        )
    pl.semaphore_wait(barrier, 3)
    vec_copy = remote(s.vec.at[c], s.vec.at[c], s.vec_sem.at[0], s.vec_sem.at[1], pair)
    vec_copy.start()

    attention_parts = []
    for g in range(STEPS):
        for k in range(3):
            start = k * D + g * GROUP
            attention_parts.append(
                (i.first.at[:, start : start + GROUP], s.w_qkv.at[g, :, k * GROUP : (k + 1) * GROUP])
            )
        attention_parts.append((i.first.at[g * GROUP : (g + 1) * GROUP, 3 * D :], s.w_out.at[g]))
    mlp_parts = []
    for j in range(CHUNKS):
        here = slice(j * CHUNK, (j + 1) * CHUNK)
        mlp_parts.append((i.first.at[:, here], s.w1.at[j]))
        mlp_parts.append((i.second.at[here], s.w2.at[j]))
    merge_parts = []
    for g in range(STEPS):
        here = slice(g * GROUP, (g + 1) * GROUP)
        merge_parts.append((i.second.at[: 2 * D, here], s.w_merge.at[:, here]))

    def load(parts, got):
        for k, (source, target) in enumerate(parts):
            local(source, target, got.at[k]).start()

    def gifts(parts, got):
        return [
            remote(source, target, s.give_sem.at[k], got.at[k], pair)
            for k, (source, target) in enumerate(parts)
        ]

    def give(parts, got):
        for copy in gifts(parts, got):
            copy.start()

    def merge_gifts():
        return [
            remote(source, target, s.merge_sem.at[1, k], s.merge_sem.at[0, k], pair)
            for k, (source, target) in enumerate(merge_parts)
        ]

    mine = pl.ds(pl.multiple_of(c * M, 16), M)

    class Delivery:
        def __init__(self, section, item, source, target):
            self.here = c == section
            self.ends = source, target
            self.sems = s.give_out.at[section, item], s.give_in.at[section, item]

        def local(self):
            return local(*self.ends, self.sems[0])

        def remote(self):
            return remote(*self.ends, *self.sems, pair)

        def start(self):
            pl.when(self.here)(lambda: self.local().start())
            pl.when(jnp.logical_not(self.here))(lambda: self.remote().start())

        def wait(self):
            pl.when(self.here)(lambda: self.local().wait())
            pl.when(jnp.logical_not(self.here))(lambda: self.remote().wait_send())

        def wait_recv(self):
            pl.when(self.here)(lambda: self.remote().wait_recv())

    def deliver_rows(section, item, source):
        target = (o.left, o.left_b, o.right_b)[item]
        return Delivery(section, item, source, target.at[mine])

    def deliver_vecs(section, source):
        return Delivery(section, 3, source, o.vecs.at[c])

    def deliver_right(section, source, where=range(4)):
        return [Delivery(section, 4 + k, source.at[k], o.right.at[k, mine]) for k in where]

    def deliver_hidden(section, source, where):
        return [Delivery(section, 8 + k, source.at[k], o.hidden.at[k, mine]) for k in where]

    def start_all(copies):
        for copy in copies:
            copy.start()

    def wait_all(copies):
        for copy in copies:
            copy.wait()

    @pl.when(c == 0)
    def _():
        @pl.when(lower)
        def _():
            start_all(merge_gifts())
            for k, (source, target) in enumerate(merge_parts):
                local(source, target, s.merge_sem.at[0, k]).start()

        @pl.when(upper)
        def _():
            give(attention_parts, s.attention_sem)

        load(attention_parts, s.attention_sem)

    @pl.when(c == 1)
    def _():
        give(mlp_parts, s.mlp_sem)
        load(mlp_parts, s.mlp_sem)

    def arrived(target, sem):
        local(target, target, sem).wait()

    def attention_weights(g):
        for k in range(3):
            arrived(s.w_qkv.at[g, :, k * GROUP : (k + 1) * GROUP], s.attention_sem.at[4 * g + k])
        arrived(s.w_out.at[g], s.attention_sem.at[4 * g + 3])

    def mlp_weights(j):
        arrived(s.w1.at[j], s.mlp_sem.at[2 * j])
        arrived(s.w2.at[j], s.mlp_sem.at[2 * j + 1])

    for copy in consts:
        copy.wait()

    def outer(ri):
        block = s.hidden.at[ri // 2] if ri < 8 else s.slope.at[0]
        return block[:INNER, ri % 2 * OFFSETS : (ri % 2 + 1) * OFFSETS]

    def inner(ci):
        block = s.hidden.at[ci // 2] if ci < 8 else s.slope.at[0]
        return block[ci % 2 * 128 : (ci % 2 + 1) * 128, 2 * OFFSETS :]

    s.table[...] = jnp.zeros_like(s.table)
    s.table[:, : SPAN * SPAN] = jnp.where(lower, i.tables[0], i.tables[1])
    table = s.table[...]
    wide = jnp.concatenate([split_dot(table, outer(ri), dot_nt) for ri in range(WIN)], 0)
    s.rel[...] = jnp.zeros_like(s.rel)
    for ci in range(WIN):
        rows = split_dot(wide, inner(ci), dot_nt)
        for ri in range(WIN):
            s.rel[pl.ds(ri * WIN + ci, HEADS, stride=ROWS), :] = rows[ri * HEADS : (ri + 1) * HEADS]

    closed = dot(i.blank[...].astype(F32).astype(BF16), i.keys[...])
    at_row = lax.broadcasted_iota(jnp.int32, (ROWS, 128), 0)
    at_lane = lax.broadcasted_iota(jnp.int32, (ROWS, 128), 1)
    own = jnp.where(at_row == at_lane, 1.0, 0.0)
    for k in range(WINS):
        found = []
        for rolled in range(2):
            for core in range(2):
                crop, part = (WINS * core + k) // 2, (WINS * core + k) % 2
                start = (2 * rolled + part) * 128
                found.append((closed[crop : crop + 1, start : start + 128], i.regions[2 * rolled + part]))
        near = [[jnp.where(c == 0, found[2 * t][u], found[2 * t + 1][u]) for u in range(2)] for t in range(2)]
        row, region = [jnp.where(lower, near[0][u], near[1][u]) for u in range(2)]
        s.mask[k] = region * jnp.maximum(1.0 - row, own)

    @pl.when(upper)
    def _():
        cot.wait()
        for crop in range(WINS):
            cotangent_copy(crop).wait()
            term = dot(s.mixed[:, crop * 256 : crop * 256 + TOK], s.cotangent[...])
            if crop == 0:
                s.acc[...] = term
            else:
                s.acc[...] += term
            if crop + 1 < WINS:
                cotangent_copy(crop + 1).start()
        s.grad_m[...] = s.acc[...].astype(BF16)
        deliver_rows(1, 2, s.grad_m).start()

    arrived(s.vec.at[1 - c], s.vec_sem.at[1])
    vec_a, vec_m = s.vec.at[0], s.vec.at[1]

    def merge_saved():
        return [
            local(s.hidden.at[2 + k], o.tokens.at[k], s.out_sem.at[1 + k]) for k in range(2)
        ] + deliver_hidden(0, s.hidden, range(2))

    @pl.when(lower)
    def _():
        for copy in picks:
            copy.wait()
        gain = jnp.concatenate([vec_a[1:2], vec_a[2:3]], 1)
        shift = jnp.concatenate([vec_a[7:8], vec_a[8:9]], 1)
        area = 4 * TOK
        for k in range(WINS):
            rows = slice(k * ROWS, (k + 1) * ROWS)
            half = lax.rem(c + k, 2)
            token_copy(k).wait()
            picked = dot(s.slope[1 + half, :, :area], s.tokens[k % 2])
            last = s.slope[3, pl.ds(pl.multiple_of(half * ROWS, 16), ROWS), :area]
            picked = [picked[t * ROWS : (t + 1) * ROWS] for t in range(3)] + [dot(last, s.tokens[k % 2])]
            if k + 2 < WINS:
                token_copy(k + 2).start()
            merged = jnp.concatenate(picked, 1)
            s.hidden[2, rows] = merged[:, :D].astype(BF16)
            s.hidden[3, rows] = merged[:, D:].astype(BF16)
            unit, _ = norm_parts(merged)
            normed = (unit * gain + shift).astype(BF16)
            s.hidden[0, rows] = normed[:, :D]
            s.hidden[1, rows] = normed[:, D:]
        start_all(merge_saved())

        @pl.when(c == 0)
        def _():
            give(attention_parts, s.attention_sem)


        for g in range(STEPS):
            here = slice(g * GROUP, (g + 1) * GROUP)
            arrived(s.w_merge.at[:, here], s.merge_sem.at[0, g])
            s.x[:, here] = dot(s.hidden[0], s.w_merge[:D, here]) + dot(s.hidden[1], s.w_merge[D:, here])

    shared = pl.ds(pl.multiple_of((1 - c) * (WINS - 1) * ROWS, 16), ROWS)
    shared_copy = remote(
        s.hop_out.at[shared], s.hop_out.at[M:], s.hop_sem.at[0], s.hop_sem.at[1], pair
    )

    def hop_copy(target):
        return remote(s.grad_a, target, s.hop_sem.at[2], s.hop_sem.at[3], across)

    def hop(target):
        shared_copy.start()
        near = dot(s.roll[:, :M], s.hop_out[:M])
        shared_copy.wait_recv()
        s.grad_a[...] = (near + dot(s.roll[:, M:], s.hop_out[M:])).astype(BF16)
        hop_copy(target).start()
        shared_copy.wait_send()

    @pl.when(upper)
    def _():
        hop_copy(s.grad_a).wait_recv()
        s.x[...] = s.grad_a[...].astype(F32)

    s.mid[...] = attention_forward(s, vec_a, attention_weights).astype(BF16)
    normed_out = deliver_rows(0, 0, s.normed)
    mixed_out = deliver_rows(0, 1, s.mixed)
    normed_out.start()
    mixed_out.start()
    normed_out.wait()

    @pl.when(lower)
    def _():
        wait_all(merge_saved())

    s.hop_out[:M] = mlp_forward(s, vec_m, mlp_weights).astype(BF16)
    normed_out = deliver_rows(1, 0, s.normed)
    normed_out.start()

    over = range(RELAY // PER)

    def hidden_over(k, core):
        rows = pl.ds(pl.multiple_of(core * M, 16), M)
        return remote(
            s.hidden.at[k], o.hidden.at[k, rows], s.over_sem.at[k], s.over_in.at[core, k], (2, w_at)
        )

    def output_copy(owner):
        wide = D // 4
        source = s.hop_out.at[:M, owner * wide : (owner + 1) * wide]
        return (
            local(source, o.outs.at[c], s.piece_sem.at[owner]),
            remote(source, o.outs.at[c], s.piece_sem.at[owner], s.outs_in.at[c], (owner, w_at)),
        )

    hidden_upper = deliver_hidden(1, s.hidden, range(4))
    hidden_lower = deliver_hidden(1, s.hidden, range(RELAY // PER, 4))
    grad_m_out = deliver_rows(1, 2, s.grad_m)

    @pl.when(lower)
    def _():
        hop(s.grad_a)
        start_all(hidden_lower)
        hop_copy(s.grad_a).wait_send()
        for k in over:
            hidden_over(k, c).start()
        hop_copy(s.grad_m).wait_recv()
        grad_m_out.start()

    @pl.when(upper)
    def _():
        start_all(hidden_upper)
        for owner in range(4):
            here, there = output_copy(owner)
            pl.when(p == owner)(here.start)
            pl.when(p != owner)(there.start)

    s.grad_a[...] = mlp_backward(s, vec_m, s.vecs_m).astype(BF16)
    right_m_out = deliver_right(1, s.slope)
    vecs_m_out = deliver_vecs(1, s.vecs_m)
    start_all(right_m_out)
    vecs_m_out.start()

    @pl.when(lower)
    def _():
        wait_all(hidden_lower)
        for k in over:
            hidden_over(k, c).wait_send()

    @pl.when(upper)
    def _():
        wait_all(hidden_upper)

    grad_a_out = Delivery(0, 4 + 3, s.grad_a, o.right.at[3, mine])
    grad_a_out.start()
    grad_out = attention_backward(s, vec_a, s.hidden, s.vecs_a)
    grad_a_out.wait()

    @pl.when(upper)
    def _():
        for owner in range(4):
            here, there = output_copy(owner)
            pl.when(p == owner)(here.wait)
            pl.when(p != owner)(there.wait_send)

    s.hop_out[:M] = grad_out.astype(BF16)
    table_out = local(s.rel, o.table, s.out_sem.at[3])
    right_a_out = [deliver_rows(0, 2, s.hop_out.at[:M])] + deliver_right(0, s.hidden, range(3))
    vecs_a_out = deliver_vecs(0, s.vecs_a)

    def merged_copy(owner):
        return local(s.slope.at[owner, :, : D // 2], o.merged.at[owner], s.piece_sem.at[owner])

    @pl.when(upper)
    def _():
        hop(s.grad_m)
        start_all(right_a_out)
        table_out.start()
        vecs_a_out.start()
        hop_copy(s.grad_m).wait_send()

    @pl.when(lower)
    def _():
        saved = [
            local(o.tokens.at[k], s.qkv.at[k], s.out_sem.at[1 + k]) for k in range(2)
        ]
        start_all(saved)
        start_all(right_a_out)
        table_out.start()
        wait_all(right_m_out)
        halves = [s.acc, s.inverse]
        for k in range(4):
            rows = slice(k * CHUNK, (k + 1) * CHUNK)
            here = slice(k % 2 * CHUNK, (k % 2 + 1) * CHUNK)
            halves[k // 2][:, here] = dot_nt(s.hop_out[:M], s.w_merge[rows])
        wait_all(saved)
        gain = jnp.concatenate([vec_a[1:2], vec_a[2:3]], 1)
        values = jnp.concatenate([s.qkv[0], s.qkv[1]], 1).astype(F32)
        grad_in, gain_grad, shift_grad = norm_backward(
            jnp.concatenate([s.acc[...], s.inverse[...]], 1), values, gain
        )
        wide = D // 8
        for owner in range(4):
            for part in range(4):
                start = part * (D // 2) + owner * wide
                s.slope[owner, :, part * wide : (part + 1) * wide] = grad_in[
                    :, start : start + wide
                ].astype(BF16)
            merged_copy(owner).start()
        s.vecs_a[1:2] = gain_grad[:, :D]
        s.vecs_a[2:3] = gain_grad[:, D:]
        s.vecs_a[7:8] = shift_grad[:, :D]
        s.vecs_a[8:9] = shift_grad[:, D:]
        vecs_a_out.start()
        for owner in range(4):
            merged_copy(owner).wait()

    @pl.when(upper)
    def _():
        wait_all(right_m_out)

    wait_all(right_a_out + [table_out, vecs_a_out, vecs_m_out, normed_out, mixed_out, grad_m_out])
    given = [deliver_rows(0, 0, s.normed), mixed_out, vecs_a_out, grad_a_out] + right_a_out
    given += [normed_out, grad_m_out, vecs_m_out] + right_m_out
    for copy in given:
        copy.wait_recv()

    @pl.when(lower)
    def _():
        for copy in deliver_hidden(0, s.hidden, range(2)) + hidden_lower:
            copy.wait_recv()

    @pl.when(upper)
    def _():
        for copy in hidden_upper:
            copy.wait_recv()

    @pl.when(p == 2)
    def _():
        for k in over:
            for core in range(2):
                hidden_over(k, core).wait_recv()

    for source in (2, 3):

        @pl.when(p != source)
        def _(source=source):
            wide = D // 4
            remote(
                s.hop_out.at[:M, :wide], o.outs.at[source % 2], s.piece_sem.at[0], s.outs_in.at[source % 2], (source, w_at)
            ).wait_recv()

    vec_copy.wait_send()

    @pl.when(c == 0)
    def _():
        for copy in gifts(attention_parts, s.attention_sem):
            copy.wait_send()

        @pl.when(lower)
        def _():
            for copy in merge_gifts():
                copy.wait_send()

    @pl.when(c == 1)
    def _():
        for copy in gifts(mlp_parts, s.mlp_sem):
            copy.wait_send()


def forward_backward(page_tokens, blank, cotangent, first, second, gains, biases, tables):
    channels = page_tokens.shape[-1]
    crops = blank.shape[0]
    rolls = np.stack([hop_matrix(False), hop_matrix(True)])
    operands = {
        "tokens": jnp.transpose(page_tokens, (0, 2, 1, 3)).reshape(crops, 4 * TOK, channels),
        "cotangent": cotangent,
        "first": first,
        "second": second,
        "pack": jnp.asarray(offset_pack(), BF16),
        "roll": jnp.asarray(rolls, BF16),
        "pick": jnp.asarray(np.pad(merge_matrix(), ((0, 0), (0, 0), (0, D - 4 * TOK))), BF16),
        "cot": jnp.asarray(cotangent_matrix(), BF16),
        "gains": jnp.transpose(gains, (1, 0, 2)),
        "biases": jnp.transpose(biases, (1, 0, 2)),
        "blank": blank,
        "tables": tables,
        "keys": jnp.asarray(key_matrix(), BF16),
        "regions": jnp.asarray(region_masks(), F32),
    }
    in_vmem = ("gains", "biases", "blank", "tables", "keys", "regions")
    four = (4, M, D)
    outs = {
        "left": ((2 * M, D), BF16),
        "left_b": ((2 * M, D), BF16),
        "right_b": ((2 * M, D), BF16),
        "right": ((4, 2 * M, D), BF16),
        "hidden": ((4, 2 * M, D), BF16),
        "vecs": ((2, 16, D), F32),
        "table": ((HEADS * ROWS, 128), F32),
        "outs": ((2, M, D // 4), BF16),
        "merged": ((4, M, D // 2), BF16),
        "tokens": ((2, M, D), BF16),
    }
    scratch = {
        "w_qkv": pltpu.VMEM((STEPS, D, 3 * GROUP), BF16),
        "w_out": pltpu.VMEM((STEPS, GROUP, D), BF16),
        "w1": pltpu.VMEM((CHUNKS, D, CHUNK), BF16),
        "w2": pltpu.VMEM((CHUNKS, CHUNK, D), BF16),
        "w_merge": pltpu.VMEM((2 * D, D), BF16),
        "x": pltpu.VMEM((M, D), F32),
        "normed": pltpu.VMEM((M, D), BF16),
        "mixed": pltpu.VMEM((M, D), BF16),
        "qkv": pltpu.VMEM((3, M, D), BF16),
        "exps": pltpu.VMEM((WINS, HEADS, ROWS, 128), BF16),
        "inverse": pltpu.VMEM((M, D), F32),
        "mid": pltpu.VMEM((M, D), BF16),
        "hidden": pltpu.VMEM(four, BF16),
        "slope": pltpu.VMEM(four, BF16),
        "pre": pltpu.VMEM((2, M, CHUNK), F32),
        "acc": pltpu.VMEM((M, D), F32),
        "hop_out": pltpu.VMEM((M + ROWS, D), BF16),
        "grad_m": pltpu.VMEM((M, D), BF16),
        "grad_a": pltpu.VMEM((M, D), BF16),
        "rel": pltpu.VMEM((HEADS * ROWS, 128), F32),
        "mask": pltpu.VMEM((WINS, ROWS, 128), F32),
        "vec": pltpu.VMEM((2, 16, D), F32),
        "vecs_a": pltpu.VMEM((16, D), F32),
        "vecs_m": pltpu.VMEM((16, D), F32),
        "tokens": pltpu.VMEM((2, 4 * TOK, channels), BF16),
        "table": pltpu.VMEM((HEADS, OFFSETS), F32),
        "cotangent": pltpu.VMEM((TOK, D), BF16),
        "roll": pltpu.VMEM((M, M + ROWS), BF16),
        "const_sem": DMA((7,)),
        "pick_sem": DMA((4,)),
        "token_sem": DMA((2,)),
        "vec_sem": DMA((2,)),
        "attention_sem": DMA((4 * STEPS,)),
        "mlp_sem": DMA((2 * CHUNKS,)),
        "merge_sem": DMA((2, STEPS)),
        "give_sem": DMA((16,)),
        "out_sem": DMA((4,)),
        "give_out": DMA((2, 12)),
        "give_in": DMA((2, 12)),
        "over_sem": DMA((4,)),
        "over_in": DMA((2, 4)),
        "outs_in": DMA((2,)),
        "piece_sem": DMA((4,)),
        "hop_sem": DMA((6,)),
    }
    found = pl.pallas_call(
        functools.partial(main_kernel, tuple(operands), tuple(outs), tuple(scratch)),
        in_specs=[IN_VMEM if k in in_vmem else ANYWHERE for k in operands],
        out_specs=[ANYWHERE] * len(outs),
        out_shape=[shape_of(*value) for value in outs.values()],
        scratch_shapes=list(scratch.values()),
        compiler_params=pltpu.CompilerParams(
            collective_id=1, has_side_effects=True, vmem_limit_bytes=61 * 1024 * 1024
        ),
        name="forward_backward",
    )(*operands.values())
    return dict(zip(outs, found))


PIECES = 2 * HALF
AHEAD = 4
RING = AHEAD + 2
LAG = 2
LEFT = PIECES
SLOTS = PIECES + 4
OWN_PIECES = (HALF + HALF // 2, 2 * HALF - RELAY, HALF + RELAY, 2 * HALF)
EARLY = AHEAD + 1


def bit_reversed(index, bits):
    return sum(((index >> b) & 1) << (bits - 1 - b) for b in range(bits))


def by_device(p, values):
    found = values[-1]
    for index in range(len(values) - 2, -1, -1):
        found = jnp.where(p == index, values[index], found)
    return found


def reduce_kernel(bits, names, *refs):
    refs = list(refs)
    count = 1 << bits
    share = D // count
    quarter = count // 4
    i = Refs(names, refs[: len(names)])
    refs = refs[len(names) :]
    first_ref, second_ref, vecs_ref, tokens_ref, tables_ref = refs[:5]
    refs = refs[5:]
    lhs_in, lhs, rhs, vec_in, vec_own, relay, score, unroll, inner, outer, table, table_recv, send, keep, whole, merged = refs[:16]
    refs = refs[16:]
    recv = refs[:bits]
    vec_recv = refs[bits : 2 * bits]
    (
        row_sem,
        stage_send,
        stage_recv,
        vec_send_sem,
        vec_recv_sem,
        table_send_sem,
        table_recv_sem,
        const_sem,
        cross_local,
        cross_send,
        cross_recv,
        relay_send,
        relay_recv,
        ready,
    ) = refs[2 * bits :]

    p = lax.axis_index("pipe")
    w = lax.axis_index("wide")
    c = lax.rem(p, 2)
    upper = p >= 2
    pair = p + 1 - 2 * c
    across = lax.rem(p + 2, 4)
    partner = []
    mine = []
    for s in range(bits):
        bit = lax.rem(w // (1 << s), 2)
        mine.append(bit)
        partner.append(w + (1 << s) * (1 - 2 * bit))

    barrier = pltpu.get_barrier_semaphore()
    pl.semaphore_signal(barrier, inc=1, device_id=(pair, w), device_id_type=MESH)
    for s in range(bits):
        pl.semaphore_signal(barrier, inc=1, device_id=(p, partner[s]), device_id_type=MESH)

    @pl.when(upper)
    def _():
        for other in (0, 1):
            pl.semaphore_signal(barrier, inc=1, device_id=(other, w), device_id_type=MESH)
        pl.semaphore_wait(barrier, 1 + bits)

    @pl.when(jnp.logical_not(upper))
    def _():
        pl.semaphore_wait(barrier, 3 + bits)
        for other in (2, 3):
            pl.semaphore_signal(ready, inc=1, device_id=(other, w), device_id_type=MESH)

    pieces = by_device(p, OWN_PIECES)

    def columns(ref, j):
        return ref.at[j // PER, :, j % PER * PIECE : (j % PER + 1) * PIECE]

    def sources(index):
        found = [(LEFT, i.left, lhs_in.at[0])]
        found += [(j, columns(i.right, j), rhs.at[j]) for j in range(HALF)]
        if index % 2 == 0:
            found.insert(AHEAD + 1, (LEFT + 1, i.left_b, lhs_in.at[1]))
        where = ((0, HALF // 2), (RELAY, HALF), (0, RELAY), (0, HALF))[index]
        more = [(LEFT + 2, i.right_b, lhs_in.at[2])]
        more += [(HALF + j, columns(i.hidden, j), rhs.at[HALF + j]) for j in range(*where)]
        return more + found if index == 2 else found + more

    def issue(early):
        part = slice(0, EARLY) if early else slice(EARLY, None)
        for index in range(4):

            @pl.when(p == index)
            def _(index=index):
                for slot, source, target in sources(index)[part]:
                    pltpu.make_async_copy(source, target, row_sem.at[slot]).start()

    issue(True)
    pltpu.make_async_copy(i.vecs, vec_in, row_sem.at[LEFT + 3]).start()
    pltpu.make_async_copy(i.table, score, const_sem.at[0]).start()
    pltpu.make_async_copy(i.inner, inner, const_sem.at[1]).start()
    pltpu.make_async_copy(i.outer, outer, const_sem.at[2]).start()

    @pl.when(p == 2)
    def _():
        pltpu.make_async_copy(i.unroll, unroll, const_sem.at[3]).start()

    def token_copy(source, target, to):
        return pltpu.make_async_remote_copy(
            merged.at[target],
            tokens_ref.at[source],
            cross_send.at[target],
            cross_recv.at[source],
            device_id=(to, w),
            device_id_type=MESH,
        )

    def token_own(index):
        return pltpu.make_async_copy(merged.at[index], tokens_ref.at[index], cross_local)

    merged_in = pltpu.make_async_copy(i.merged, merged, const_sem.at[4])

    @pl.when(jnp.logical_not(upper))
    def _():
        merged_in.start()

    def rows_wait(slot, target):
        pltpu.make_async_copy(target, target, row_sem.at[slot]).wait()

    def turn(k, unrolled):
        rows_wait(LEFT + k, lhs_in.at[k])
        if unrolled:
            pltpu.make_async_copy(i.unroll, unroll, const_sem.at[3]).wait()
        per = max(1, 128 // share)
        at_row = lax.broadcasted_iota(jnp.int32, (128, 128), 0)
        at_lane = lax.broadcasted_iota(jnp.int32, (128, 128), 1)
        unit = jnp.where(at_row == at_lane, 1.0, 0.0).astype(BF16)
        for block in range(D // 128):
            flipped = dot_nt(unit, lhs_in[k, :, block * 128 : (block + 1) * 128]).astype(BF16)
            if unrolled:
                flipped = dot(flipped, unroll[...]).astype(BF16)
            if share >= 128:
                at = bit_reversed(block * 128 // share, bits)
                start = block * 128 % share
                lhs[k, at // quarter, at % quarter, start : start + 128] = flipped
            else:
                for q in range(per):
                    at = bit_reversed(block * per + q, bits)
                    lhs[k, at // quarter, at % quarter] = flipped[q * share : (q + 1) * share]

    def swapped(t):
        return (4 - lax.rem(t, 4)) // 4

    def stage_of(s, t):
        if s >= 2:
            return mine[s], partner[s]
        odd = swapped(t)
        return (
            mine[s] + odd * (mine[1 - s] - mine[s]),
            partner[s] + odd * (partner[1 - s] - partner[s]),
        )

    def stage_copy(s, t):
        j = piece(t)
        half, to = stage_of(s, t)
        if s == 0:
            source = send.at[lax.rem(t, RING)]
        elif s == 1:
            source = recv[0].at[j, 1 - half]
        else:
            width = count >> (s + 1)
            source = recv[s - 1].at[j, pl.ds((1 - half) * width, width)]
        return pltpu.make_async_remote_copy(
            source,
            recv[s].at[j],
            stage_send.at[s, j],
            stage_recv.at[s, j],
            device_id=(p, to),
            device_id_type=MESH,
        )

    def send_first(t):
        j = piece(t)
        slot = lax.rem(t, RING)

        @pl.when((j == 0) & (p == 2))
        def _():
            turn(0, False)

        @pl.when((j == HALF - PER) & (c == 0))
        def _():
            turn(1, False)

        @pl.when(j == by_device(p, (HALF, HALF + RELAY, PIECES, HALF)))
        def _():
            turn(2, False)

        @pl.when(t >= RING)
        def _():
            stage_copy(0, t - RING).wait_send()

        rows_wait(j, rhs.at[j])
        odd = swapped(t)
        sel = jnp.where(j < HALF - PER, 0, jnp.where(j < HALF, 1 - c, 2))
        product = dot(lhs[sel].reshape(D, 2 * M), rhs[j])
        for high in range(2):
            for low in range(2):
                bit = (1 - odd) * high + odd * low
                part = (1 - odd) * low + odd * high
                keeps = 1 - (bit - mine_first(odd)) * (bit - mine_first(odd))
                rows = (2 * high + low) * (D // 4)
                whole[2 * keeps + part] = product[rows : rows + D // 4].reshape(quarter, share, PIECE)
        send[slot] = whole[:2].astype(BF16)
        keep[slot] = whole[2:]
        stage_copy(0, t).start()

    def mine_first(odd):
        return mine[0] + odd * (mine[1] - mine[0])

    def store_out(j, values):
        @pl.when(j < HALF)
        def _():
            first_ref[:, pl.ds(pl.multiple_of(j * PIECE, PIECE), PIECE)] = values

        @pl.when(j >= HALF)
        def _():
            turned = jnp.transpose(values)

            @pl.when(p == 2)
            def _():
                relay[j - HALF] = turned

            @pl.when(p != 2)
            def _():
                second_ref[pl.ds(pl.multiple_of((j - HALF) * PIECE, PIECE), PIECE)] = turned

    def take(s, t):
        j = piece(t)
        stage_copy(s, t).wait_recv()
        half, _ = stage_of(s, t)
        if s == 0:
            kept = keep[lax.rem(t, RING)]
        elif s == 1:
            kept = recv[0][j, half].astype(F32)
        else:
            width = count >> (s + 1)
            kept = recv[s - 1][j, pl.ds(half * width, width)].astype(F32)
        total = kept + recv[s][j].astype(F32)
        if s == bits - 1:
            store_out(j, total[0])
        else:
            recv[s][j] = total.astype(BF16)
            stage_copy(s + 1, t).start()

    def piece(t):
        return by_device(
            p,
            (
                t,
                jnp.where(t < HALF, t, t + RELAY),
                jnp.where(t < RELAY, t + HALF, t - RELAY),
                t,
            ),
        )

    @pl.when(p == 2)
    def _():
        turn(2, True)

    @pl.when(p != 2)
    def _():
        turn(0, False)

    issue(False)

    for index in range(2):

        @pl.when(p == index)
        def _(index=index):
            merged_in.wait()
            token_own(index).start()
            for target in range(4):
                if target != index:
                    token_copy(index, target, target).start()

    lax.fori_loop(0, AHEAD, lambda t, _: (send_first(t), 0)[1], 0)

    def vec_copy(s):
        width = count >> (s + 1)
        held = vec_own if s == 0 else vec_recv[s - 1]
        return pltpu.make_async_remote_copy(
            held.at[pl.ds((1 - mine[s]) * width, width)],
            vec_recv[s],
            vec_send_sem.at[s],
            vec_recv_sem.at[s],
            device_id=(p, partner[s]),
            device_id_type=MESH,
        )

    def vec_start():
        rows_wait(LEFT + 3, vec_in)
        both = jnp.concatenate([vec_in[0] + vec_in[1], jnp.zeros((112, D), F32)], 0)
        per = max(1, 128 // share)
        for block in range(D // 128):
            flipped = jnp.transpose(both[:, block * 128 : (block + 1) * 128])
            if share >= 128:
                at = bit_reversed(block * 128 // share, bits)
                inside = block * 128 % share
                vec_own[at, inside : inside + 128] = flipped
            else:
                for q in range(per):
                    at = bit_reversed(block * per + q, bits)
                    vec_own[at] = flipped[q * share : (q + 1) * share]
        vec_copy(0).start()

    def vec_step(s):
        width = count >> (s + 1)
        vec_copy(s).wait_recv()
        held = vec_own if s == 0 else vec_recv[s - 1]
        total = held[pl.ds(mine[s] * width, width)] + vec_recv[s][...]
        if s == bits - 1:
            vecs_ref[...] = total[0]
        else:
            vec_recv[s][...] = total
            vec_copy(s + 1).start()

    def table_copy(s):
        to = (pair, w) if s == 0 else (p, partner[s - 1])
        return pltpu.make_async_remote_copy(
            table.at[s],
            table_recv.at[s],
            table_send_sem.at[s],
            table_recv_sem.at[s],
            device_id=to,
            device_id_type=MESH,
        )

    def table_start():
        pltpu.make_async_copy(i.table, score, const_sem.at[0]).wait()
        pltpu.make_async_copy(i.inner, inner, const_sem.at[1]).wait()
        pltpu.make_async_copy(i.outer, outer, const_sem.at[2]).wait()
        by_row = None
        for ci in range(WIN):
            rows = jnp.concatenate(
                [score[pl.ds(ri * WIN + ci, HEADS, stride=ROWS), :] for ri in range(WIN)], 0
            )
            term = split_dot(rows, inner[ci])
            by_row = term if by_row is None else by_row + term
        total = None
        for ri in range(WIN):
            term = split_dot(by_row[ri * HEADS : (ri + 1) * HEADS], outer[ri])
            total = term if total is None else total + term
        table[0] = total
        table_copy(0).start()

    def table_cross():
        x = p // 2
        return pltpu.make_async_remote_copy(
            table.at[bits + 1],
            tables_ref.at[x],
            table_send_sem.at[bits + 1],
            table_recv_sem.at[bits + 1],
            device_id=(across, w),
            device_id_type=MESH,
        )

    def table_step(s):
        table_copy(s).wait_recv()
        table[s + 1] = table[s] + table_recv[s]
        if s < bits:
            table_copy(s + 1).start()
        else:
            tables_ref[p // 2] = table[s + 1]

            @pl.when(jnp.logical_not(upper))
            def _():
                table_cross().start()

    def relay_copy(k):
        return pltpu.make_async_remote_copy(
            relay.at[k],
            second_ref.at[k * PIECE : (k + 1) * PIECE],
            relay_send.at[k],
            relay_recv.at[k],
            device_id=(1, w),
            device_id_type=MESH,
        )

    vec_start()
    table_start()

    def body(t, carry):
        for s in range(bits):
            at = t - LAG * s

            @pl.when((at >= 0) & (at < pieces))
            def _(s=s, at=at):
                take(s, at)
                if s == 0:

                    @pl.when(t + AHEAD < pieces)
                    def _():
                        send_first(t + AHEAD)

        for s in range(bits):

            @pl.when(t == 2 * s + 2)
            def _(s=s):
                vec_step(s)

        for s in range(bits + 1):

            @pl.when(t == 2 * s + 2)
            def _(s=s):
                table_step(s)

        @pl.when(upper & (t == RELAY + LAG * (bits - 1)))
        def _():
            pl.semaphore_wait(ready, 2)
            table_cross().start()

            @pl.when(p == 2)
            def _():
                for k in range(RELAY):
                    relay_copy(k).start()

        return carry

    lax.fori_loop(0, pieces + LAG * (bits - 1), body, 0)

    def clear(j, carry):
        second_ref[pl.ds(pl.multiple_of(j * PIECE, PIECE), PIECE)] = jnp.zeros((PIECE, share), F32)
        return carry

    lax.fori_loop(by_device(p, (HALF // 2, HALF, 0, HALF)), HALF, clear, 0)

    def drain(t, carry):
        @pl.when(t >= pieces - RING)
        def _():
            stage_copy(0, t).wait_send()

        for s in range(1, bits):
            stage_copy(s, t).wait_send()
        return carry

    lax.fori_loop(0, pieces, drain, 0)
    for s in range(bits):
        vec_copy(s).wait_send()
    for s in range(bits + 1):
        table_copy(s).wait_send()
    table_cross().wait()

    for index in range(4):

        @pl.when(p == index)
        def _(index=index):
            if index < 2:
                token_own(index).wait()
                for target in range(4):
                    if target != index:
                        token_copy(index, target, target).wait_send()
            for source in range(2):
                if source != index:
                    token_copy(source, index, source).wait_recv()
            if index == 2:
                for k in range(RELAY):
                    relay_copy(k).wait_send()
            if index == 1:
                for k in range(RELAY):
                    relay_copy(k).wait_recv()


def reduce_gradients(made, count):
    bits = count.bit_length() - 1
    share = D // count
    anywhere = pl.BlockSpec(memory_space=pl.ANY)
    in_vmem = pl.BlockSpec(memory_space=pltpu.VMEM)
    inner, outer = offset_blocks()
    flat = (HEADS * ROWS, 128)
    operands = {name: made[name] for name in made if name not in ("tokens", "outs")}
    operands["unroll"] = jnp.asarray(unroll_matrix(), BF16)
    operands["inner"] = jnp.asarray(inner, BF16)
    operands["outer"] = jnp.asarray(outer, BF16)
    merged = made["merged"]
    dma = pltpu.SemaphoreType.DMA
    halves = [(2, count // 4)] + [(count >> (s + 1),) for s in range(1, bits)]
    return pl.pallas_call(
        functools.partial(reduce_kernel, bits, tuple(operands)),
        in_specs=[anywhere] * len(operands),
        out_specs=[in_vmem] * 3 + [anywhere] + [in_vmem],
        out_shape=[
            shape_of((share, FF), F32),
            shape_of((FF, share), F32),
            shape_of((share, 128), F32),
            shape_of((2,) + merged.shape[1:], BF16),
            shape_of((2, HEADS, OFFSETS), F32),
        ],
        scratch_shapes=[
            pltpu.VMEM((3, 2 * M, D), BF16),
            pltpu.VMEM((3, 4, count // 4, share, 2 * M), BF16),
            pltpu.VMEM((PIECES, 2 * M, PIECE), BF16),
            pltpu.VMEM((2, 16, D), F32),
            pltpu.VMEM((count, share, 128), F32),
            pltpu.VMEM((RELAY, PIECE, share), F32),
            pltpu.VMEM(flat, F32),
            pltpu.VMEM((2 * M, 2 * M), BF16),
            pltpu.VMEM(inner.shape, BF16),
            pltpu.VMEM(outer.shape, BF16),
            pltpu.VMEM((bits + 2, HEADS, OFFSETS), F32),
            pltpu.VMEM((bits + 1, HEADS, OFFSETS), F32),
            pltpu.VMEM((RING, 2, count // 4, share, PIECE), BF16),
            pltpu.VMEM((RING, 2, count // 4, share, PIECE), F32),
            pltpu.VMEM((4, count // 4, share, PIECE), F32),
            pltpu.VMEM(merged.shape, BF16),
            *[pltpu.VMEM((PIECES,) + half + (share, PIECE), BF16) for half in halves],
            *[pltpu.VMEM((count >> (s + 1), share, 128), F32) for s in range(bits)],
            dma((SLOTS,)),
            dma((bits, PIECES)),
            dma((bits, PIECES)),
            dma((bits,)),
            dma((bits,)),
            dma((bits + 2,)),
            dma((bits + 2,)),
            dma((5,)),
            dma,
            dma((4,)),
            dma((2,)),
            dma((RELAY,)),
            dma((RELAY,)),
            pltpu.SemaphoreType.REGULAR,
        ],
        compiler_params=pltpu.CompilerParams(
            collective_id=0, has_side_effects=True, vmem_limit_bytes=60 * 1024 * 1024
        ),
        name="reduce_gradients",
    )(*operands.values())


def finish_kernel(
    first_in, second_in, vecs_in, outs_in, parts_in, tables_in, order_in, split_in,
    output_ref, tokens_ref, first_out, second_out, gains_ref, biases_ref, tables_out,
    vecs_ref, outs_ref, parts_ref, tables_ref, order_ref, split_ref, first_ref, second_ref, sems,
):
    copies = [
        pltpu.make_async_copy(source, target, sems.at[k])
        for k, (source, target) in enumerate(
            (
                (parts_in, parts_ref),
                (split_in, split_ref),
                (outs_in, outs_ref),
                (order_in, order_ref),
                (tables_in, tables_ref),
                (vecs_in, vecs_ref),
                (first_in, first_ref),
                (second_in, second_ref),
            )
        )
    ]
    for copy in copies:
        copy.start()
    for copy in copies[:6]:
        copy.wait()
    on = []
    for copy, source, target in ((copies[6], first_ref, first_out), (copies[7], second_ref, second_out)):
        copy.wait()
        on.append(pltpu.make_async_copy(source, target, sems.at[8 + len(on)]))
        on[-1].start()
    tables_out[...] = tables_ref[:, :, : SPAN * SPAN]
    vecs = jnp.transpose(vecs_ref[...])
    for row in range(3):
        gains_ref[row] = vecs[row : row + 1]
    for row in range(6):
        biases_ref[row] = vecs[3 + row : 4 + row]
    channels = tokens_ref.shape[-1]
    for crop in range(WINS):
        windows = []
        for half in range(2):
            window = 2 * crop + half
            core, k = window // WINS, window % WINS
            windows.append((core, slice(k * ROWS, (k + 1) * ROWS)))
        rolled = jnp.concatenate([outs_ref[core, rows] for core, rows in windows], 0)
        output_ref[crop] = dot(order_ref[...], rolled).astype(BF16)
        total = None
        for half, (core, rows) in enumerate(windows):
            cells = jnp.concatenate(
                [parts_ref[core, rows, t * channels : (t + 1) * channels] for t in range(4)], 0
            )
            term = dot(split_ref[half], cells)
            total = term if total is None else total + term
        tokens_ref[crop] = total
    for copy in on:
        copy.wait()


def finish(out_parts, first_part, second_part, vec_part, token_parts, table_parts):
    share = first_part.shape[0]
    split = np.transpose(merge_matrix(), (0, 2, 1))
    channels = token_parts.shape[-1] // 4
    return pl.pallas_call(
        finish_kernel,
        in_specs=[ANYWHERE] * 8,
        out_specs=[IN_VMEM] * 2 + [ANYWHERE] * 2 + [IN_VMEM] * 3,
        out_shape=[
            shape_of((WINS, TOK, out_parts.shape[-1]), BF16),
            shape_of((WINS, 4 * TOK, channels), F32),
            shape_of(first_part.shape, F32),
            shape_of(second_part.shape, F32),
            shape_of((3, 1, share), F32),
            shape_of((6, 1, share), F32),
            shape_of((2, HEADS, SPAN * SPAN), F32),
        ],
        scratch_shapes=[
            pltpu.VMEM(vec_part.shape, F32),
            pltpu.VMEM(out_parts.shape, BF16),
            pltpu.VMEM(token_parts.shape, BF16),
            pltpu.VMEM(table_parts.shape, F32),
            pltpu.VMEM((TOK, 2 * ROWS), BF16),
            pltpu.VMEM(split.shape, BF16),
            pltpu.VMEM(first_part.shape, F32),
            pltpu.VMEM(second_part.shape, F32),
            DMA((10,)),
        ],
        compiler_params=pltpu.CompilerParams(vmem_limit_bytes=61 * 1024 * 1024),
        name="finish",
    )(
        first_part,
        second_part,
        vec_part,
        out_parts,
        token_parts,
        table_parts,
        jnp.asarray(output_matrix(), BF16),
        jnp.asarray(split, BF16),
    )


def padded_row(token):
    return (token // AREA) * ROWS + token % AREA


def rolled_source():
    cells = np.arange(TOK)
    rows, columns = cells // GRID_W, cells % GRID_W
    return ((rows + WIN // 2) % GRID_H) * GRID_W + (columns + WIN // 2) % GRID_W


def hop_matrix(inverse):
    source = rolled_source()
    if inverse:
        source = np.argsort(source)
    result = np.zeros((2, M, (WINS + 1) * ROWS), np.float32)
    for core in range(2):
        for k in range(WINS):
            window = WINS * core + k
            crop, part = window // 2, window % 2
            for t in range(AREA):
                token = source[part * AREA + t]
                taken = crop * 2 + token // AREA
                slot = taken - WINS * core
                if not 0 <= slot < WINS:
                    slot = WINS
                result[core, k * ROWS + t, slot * ROWS + token % AREA] = 1.0
    return result


def cotangent_matrix():
    source = rolled_source()
    result = np.zeros((2, M, 4 * 256), np.float32)
    for core in range(2):
        for k in range(WINS):
            window = WINS * core + k
            crop, part = window // 2, window % 2
            for t in range(AREA):
                result[core, k * ROWS + t, crop * 256 + source[part * AREA + t]] = 1.0
    return result


def output_matrix():
    source = rolled_source()
    result = np.zeros((TOK, 2 * ROWS), np.float32)
    for t in range(TOK):
        result[source[t], padded_row(t)] = 1.0
    return result


def offset_matrices():
    span = 2 * WIN - 1
    inner = np.zeros((WIN, 128, WIN, span), np.float32)
    outer = np.zeros((WIN, WIN, span, span, span), np.float32)
    for ci in range(WIN):
        for j in range(AREA):
            inner[ci, j, j // WIN, ci - j % WIN + WIN - 1] = 1.0
    for ri in range(WIN):
        for rj in range(WIN):
            for dc in range(span):
                outer[ri, rj, dc, ri - rj + WIN - 1, dc] = 1.0
    return (
        inner.reshape(WIN * 128, WIN * span),
        outer.reshape(WIN * WIN * span, span * span),
    )


def offset_blocks():
    inner, outer = offset_matrices()
    inner = np.pad(inner.reshape(WIN, 128, WIN * SPAN), ((0, 0), (0, 0), (0, INNER - WIN * SPAN)))
    outer = np.pad(
        outer.reshape(WIN, WIN * SPAN, SPAN * SPAN),
        ((0, 0), (0, INNER - WIN * SPAN), (0, OFFSETS - SPAN * SPAN)),
    )
    return inner, outer


def offset_pack():
    inner, outer = offset_blocks()
    result = np.zeros((WIN // 2, INNER, D), np.float32)
    for k in range(WIN):
        half = k % 2
        result[k // 2, :, half * OFFSETS : (half + 1) * OFFSETS] = outer[k]
        result[k // 2, half * 128 : (half + 1) * 128, 2 * OFFSETS :] = inner[k]
    return result


def unroll_matrix():
    source = rolled_source()
    result = np.zeros((2 * M, 2 * M), np.float32)
    for crop in range(WINS):
        for t in range(TOK):
            start = crop * 2 * ROWS
            result[start + padded_row(t), start + padded_row(source[t])] = 1.0
    return result


def merge_matrix():
    result = np.zeros((2, 4, ROWS, 2 * GRID_W, 2 * GRID_H), np.float32)
    for half in range(2):
        for part in range(4):
            right, down = part // 2, part % 2
            for t in range(AREA):
                result[half, part, t, 2 * (t % WIN) + right, 2 * (half * WIN + t // WIN) + down] = 1.0
    return result.reshape(2, 4 * ROWS, 4 * TOK)


def region_masks():
    cells = np.arange(TOK)
    rows_at, cols_at = cells // GRID_W, cells % GRID_W
    row_band = (rows_at >= GRID_H - WIN).astype(int) + (rows_at >= GRID_H - WIN // 2)
    col_band = (cols_at >= GRID_W - WIN).astype(int) + (cols_at >= GRID_W - WIN // 2)
    rolled = (row_band * 3 + col_band).reshape(2, AREA)
    result = np.zeros((4, ROWS, 128), np.float32)
    for part in range(2):
        result[part, :AREA, :AREA] = 1.0
        result[2 + part, :AREA, :AREA] = rolled[part][:, None] == rolled[part][None, :]
    return result


def key_matrix():
    source = rolled_source()
    result = np.zeros((TOK, 4, 128), np.float32)
    for part in range(2):
        for t in range(AREA):
            result[part * AREA + t, part, t] = 1.0
            result[source[part * AREA + t], 2 + part, t] = 1.0
    return result.reshape(TOK, 4 * 128)


def local(page_tokens, blank, cotangent, first, second, gains, biases, tables):
    count = lax.axis_size("wide")
    made = forward_backward(
        page_tokens, blank, cotangent, first[0], second[0], gains, biases, tables
    )
    output, token_grad, first_grad, second_grad, gain_grad, bias_grad, table_grad = finish(
        made["outs"], *reduce_gradients(made, count)
    )
    crops, rows, columns, channels = page_tokens.shape
    token_grad = token_grad.reshape(crops, columns, rows, channels // 4)
    return (
        output,
        jnp.transpose(token_grad, (0, 2, 1, 3)),
        first_grad[None],
        second_grad[None],
        jnp.transpose(gain_grad, (1, 0, 2)),
        jnp.transpose(bias_grad, (1, 0, 2)),
        table_grad,
    )


def solution(mesh):
    placed = (
        P("wide", None, None, None),
        P("wide", None),
        P("wide", None, None),
        P("pipe", None, None),
        P("pipe", None, None),
        P("pipe", None, None),
        P("pipe", None, None),
        P(),
    )
    return jax.shard_map(
        local,
        mesh=mesh,
        in_specs=placed,
        out_specs=(
            P("wide", None, "pipe"),
            P("wide", None, None, "pipe"),
            P("pipe", "wide", None),
            P("pipe", None, "wide"),
            P("pipe", None, "wide"),
            P("pipe", None, "wide"),
            P(),
        ),
        check_vma=False,
    )
```

time: 3590 us -> 310 us (0.09)
  the two profiles are of different devices: /device:TPU:15 before, /device:TPU:3 now
where the time goes in v1:
time: 310 us; the launch traced here: 305 us
  Pallas kernels  304 us (98%)
    pallas_call x1, Pallas kernels, reduce_gradients(): pl.pallas_call(functools.partial(reduce_kernel, bits, tuple(operands)), i...  180 us
    pallas_call x1, Pallas kernels, forward_backward(): pl.pallas_call(functools.partial(main_kernel, tuple(operands), tuple(outs...  118 us

profile of v1, /device:TPU:3, one launch (start us, length us, event | category | flops | bytes accessed | tf_op | source)
XLA Modules:
  0.0 304.6 jit_solution(16423680813094379389)
XLA Ops:
  0.6 117.9 %forward_backward.1 = (bf16[672,1024]{1,0:T(8,128)(2,1)}, bf16[672,1024]{1,0:T(8,128)(2,1)}, bf16[672,1024]{1,0:T(8,128)(2,1)}, bf16[4,672,1024]{2,1,0:T(8,128)(...) custom-call(bf16[3,800,512]{2,1,0:T(8,128)(2,1)} %bitcast.16, ...), custom_call_target="tpu_custom_call" | custom-call | tf_op jit(solution)/shard_map/forward_backward/pallas_call | solution.py:848
  118.5 179.9 %reduce_gradients.1 = (f32[128,4096]{1,0:T(8,128)}, f32[4096,128]{1,0:T(8,128)}, f32[128,128]{1,0:T(8,128)}, bf16[2,336,512]{2,1,0:T(8,128)(2,1)}, f32[2,32,384]{2,1,0:T(8,128)}) custom-call(bf16[672,1024]{1,0:T(8,128)(2,1)} %get-tuple-element.28.refs_0_, bf16[672,1024]{1,0:T(8,128)(2,1)} %get-tuple-element.29.refs_1_, ...), custom_call_target="tpu_custom_call" | custom-call | tf_op jit(solution)/shard_map/reduce_gradients/pallas_call | solution.py:1356
  298.4 5.9 %finish.1 = (bf16[3,200,256]{2,1,0:T(8,128)(2,1)}, f32[3,800,128]{2,1,0:T(8,128)}, f32[128,4096]{1,0:T(8,128)}, f32[4096,128]{1,0:T(8,128)}, f32[3,1,128]{2,1,0:...) custom-call(f32[128,4096]{1,0:T(8,128)} %get-tuple-element.36.first_in, f32[4096,128]{1,0:T(8,128)} %get-tuple-element.37.second_in, ...), custom_call_target="tpu_custom_call" | custom-call | tf_op jit(solution)/shard_map/finish/pallas_call | solution.py:1468

commit v2 on v1

--- a/solution.py
+++ b/solution.py
@@ -129,15 +129,20 @@
         weights(g)
         here = lanes_at(g * GROUP, GROUP)
         projected = dot(s.normed[...], s.w_qkv[g])
-        s.qkv[0, :, here] = (projected[:, :GROUP] + vec[4:5, here]).astype(BF16)
-        s.qkv[1, :, here] = projected[:, GROUP : 2 * GROUP].astype(BF16)
-        s.qkv[2, :, here] = (projected[:, 2 * GROUP :] + vec[5:6, here]).astype(BF16)
+        query = (projected[:, :GROUP] + vec[4:5, here]).astype(BF16)
+        key = projected[:, GROUP : 2 * GROUP].astype(BF16)
+        value = (projected[:, 2 * GROUP :] + vec[5:6, here]).astype(BF16)
+        for k, values in enumerate((query, key, value)):
+            s.qkv[k, :, here] = values
+        mixed = []
         for w in range(WINS):
             rows = slice(w * ROWS, (w + 1) * ROWS)
             allowed = s.mask[w] > 0.5
+            parts = []
             for part in range(GROUP // 128):
+                inside = slice(part * 128, (part + 1) * 128)
                 lanes = lanes_at(g * GROUP + part * 128, 128)
-                scores = dot_nt(s.qkv[0, rows, lanes], stacked(s.qkv[1, rows, lanes], masks, 128))
+                scores = dot_nt(query[rows, inside], stacked(key[rows, inside], masks, 128))
                 found = []
                 for h in range(4):
                     head = g * GROUP_HEADS + part * 4 + h
@@ -148,11 +153,14 @@
                     exponent = jnp.exp(one - jnp.max(one, -1, keepdims=True)).astype(BF16)
                     s.exps[w, head] = exponent
                     found.append(exponent)
-                sums = dot(jnp.concatenate(found, 1), beside_ones(s.qkv[2, rows, lanes], masks))
+                sums = dot(jnp.concatenate(found, 1), beside_ones(value[rows, inside], masks))
                 scale = 1.0 / sums[:, 128:]
                 s.inverse[rows, lanes] = scale
-                s.mixed[rows, lanes] = (sums[:, :128] * scale).astype(BF16)
-        s.acc[...] += dot(s.mixed[:, here], s.w_out[g])
+                parts.append((sums[:, :128] * scale).astype(BF16))
+            mixed.append(jnp.concatenate(parts, 1))
+        mixed = jnp.concatenate(mixed, 0)
+        s.mixed[:, here] = mixed
+        s.acc[...] += dot(mixed, s.w_out[g])
         return carry
 
     lax.fori_loop(0, STEPS, step, 0)
@@ -168,15 +176,17 @@
         mixed_grad = dot_nt(s.grad_a[...], s.w_out[g])
         scaled_grad = (mixed_grad * s.inverse[:, here]).astype(BF16)
         spread = (scaled_grad.astype(F32) * s.mixed[:, here].astype(F32)).astype(BF16)
+        query, key, value = [s.qkv[k, :, here] for k in range(3)]
+        made = []
         for w in range(WINS):
             rows = slice(w * ROWS, (w + 1) * ROWS)
+            parts = []
             for part in range(GROUP // 128):
                 inside = slice(part * 128, (part + 1) * 128)
-                lanes = lanes_at(g * GROUP + part * 128, 128)
                 grad_here = scaled_grad[rows, inside]
                 prob_grad = dot_nt(
                     jnp.concatenate([grad_here, -spread[rows, inside]], 1),
-                    beside_ones(s.qkv[2, rows, lanes], masks),
+                    beside_ones(value[rows, inside], masks),
                 )
                 found = []
                 draws = []
@@ -191,14 +201,15 @@
                         s.rel[at] += score_grad
                     found.append(exponent)
                     draws.append((score_grad * SCALE).astype(BF16))
-                query_grad = dot(jnp.concatenate(draws, 1), stacked(s.qkv[1, rows, lanes], masks, 128))
-                key_grad = dot_tn(jnp.concatenate(draws, 0), stacked(s.qkv[0, rows, lanes], masks, ROWS))
+                query_grad = dot(jnp.concatenate(draws, 1), stacked(key[rows, inside], masks, 128))
+                key_grad = dot_tn(jnp.concatenate(draws, 0), stacked(query[rows, inside], masks, ROWS))
                 value_grad = dot_tn(jnp.concatenate(found, 0), stacked(grad_here, masks, ROWS))
-                right[0, rows, lanes] = query_grad.astype(BF16)
-                right[1, rows, lanes] = key_grad[:ROWS].astype(BF16)
-                right[2, rows, lanes] = value_grad[:ROWS].astype(BF16)
-        joined = jnp.concatenate([right[k, :, here] for k in range(3)], 1)
-        s.acc[...] += dot_nt(joined, s.w_qkv[g])
+                parts.append([t[:ROWS].astype(BF16) for t in (query_grad, key_grad, value_grad)])
+            made.append([jnp.concatenate([part[k] for part in parts], 1) for k in range(3)])
+        made = [jnp.concatenate([window[k] for window in made], 0) for k in range(3)]
+        for k in range(3):
+            right[k, :, here] = made[k]
+        s.acc[...] += dot_nt(jnp.concatenate(made, 1), s.w_qkv[g])
         return carry
 
     lax.fori_loop(0, STEPS, step, 0)
@@ -345,7 +356,12 @@
         pl.semaphore_signal(
             barrier, inc=1, device_id=(lax.rem(p + step, 4), w_at), device_id_type=MESH
         )
-    pl.semaphore_wait(barrier, 3)
+    beside = []
+    for b in range(2):
+        bit = lax.rem(w_at // (1 << b), 2)
+        beside.append((pair[0], w_at + (1 << b) * (1 - 2 * bit)))
+        pl.semaphore_signal(barrier, inc=1, device_id=beside[b], device_id_type=MESH)
+    pl.semaphore_wait(barrier, 5)
     vec_copy = remote(s.vec.at[c], s.vec.at[c], s.vec_sem.at[0], s.vec_sem.at[1], pair)
     vec_copy.start()
 
@@ -372,10 +388,11 @@
             local(source, target, got.at[k]).start()
 
     def gifts(parts, got):
-        return [
-            remote(source, target, s.give_sem.at[k], got.at[k], pair)
-            for k, (source, target) in enumerate(parts)
-        ]
+        found = []
+        for k, (source, target) in enumerate(parts):
+            to = beside[k // 8] if parts is attention_parts and k % 4 == 3 else pair
+            found.append(remote(source, target, s.give_sem.at[k], got.at[k], to))
+        return found
 
     def give(parts, got):
         for copy in gifts(parts, got):
@@ -484,6 +501,10 @@
         rows = split_dot(wide, inner(ci), dot_nt)
         for ri in range(WIN):
             s.rel[pl.ds(ri * WIN + ci, HEADS, stride=ROWS), :] = rows[ri * HEADS : (ri + 1) * HEADS]
+
+    @pl.when(lower & (c == 0))
+    def _():
+        give(attention_parts, s.attention_sem)
 
     closed = dot(i.blank[...].astype(F32).astype(BF16), i.keys[...])
     at_row = lax.broadcasted_iota(jnp.int32, (ROWS, 128), 0)
@@ -519,9 +540,7 @@
     vec_a, vec_m = s.vec.at[0], s.vec.at[1]
 
     def merge_saved():
-        return [
-            local(s.hidden.at[2 + k], o.tokens.at[k], s.out_sem.at[1 + k]) for k in range(2)
-        ] + deliver_hidden(0, s.hidden, range(2))
+        return [local(s.hidden.at[k], o.tokens.at[k], s.save_sem.at[k]) for k in range(4)]
 
     @pl.when(lower)
     def _():
@@ -548,11 +567,6 @@
             s.hidden[1, rows] = normed[:, D:]
         start_all(merge_saved())
 
-        @pl.when(c == 0)
-        def _():
-            give(attention_parts, s.attention_sem)
-
-
         for g in range(STEPS):
             here = slice(g * GROUP, (g + 1) * GROUP)
             arrived(s.w_merge.at[:, here], s.merge_sem.at[0, g])
@@ -563,36 +577,51 @@
         s.hop_out.at[shared], s.hop_out.at[M:], s.hop_sem.at[0], s.hop_sem.at[1], pair
     )
 
-    def hop_copy(target):
-        return remote(s.grad_a, target, s.hop_sem.at[2], s.hop_sem.at[3], across)
+    early = pl.ds(pl.multiple_of(c * ROWS, 16), 2 * ROWS)
+    late = pl.ds(pl.multiple_of((1 - c) * 2 * ROWS, 16), ROWS)
+
+    def hop_copies(target):
+        return [
+            remote(s.grad_a.at[rows], target.at[rows], s.hop_sem.at[2 * k], s.hop_sem.at[2 * k + 1], across)
+            for k, rows in ((1, early), (2, late))
+        ]
 
     def hop(target):
+        first, last = hop_copies(target)
         shared_copy.start()
-        near = dot(s.roll[:, :M], s.hop_out[:M])
+        s.grad_a[early] = dot(s.roll[early, :M], s.hop_out[:M]).astype(BF16)
+        first.start()
+        near = dot(s.roll[late, :M], s.hop_out[:M])
         shared_copy.wait_recv()
-        s.grad_a[...] = (near + dot(s.roll[:, M:], s.hop_out[M:])).astype(BF16)
-        hop_copy(target).start()
+        s.grad_a[late] = (near + dot(s.roll[late, M:], s.hop_out[M:])).astype(BF16)
+        last.start()
         shared_copy.wait_send()
 
     @pl.when(upper)
     def _():
-        hop_copy(s.grad_a).wait_recv()
+        for copy in hop_copies(s.grad_a):
+            copy.wait_recv()
         s.x[...] = s.grad_a[...].astype(F32)
 
     s.mid[...] = attention_forward(s, vec_a, attention_weights).astype(BF16)
     normed_out = deliver_rows(0, 0, s.normed)
     mixed_out = deliver_rows(0, 1, s.mixed)
-    normed_out.start()
+
+    @pl.when(lower)
+    def _():
+        aside = local(s.normed, o.tokens.at[4], s.save_sem.at[4])
+        aside.start()
+        wait_all(merge_saved())
+        aside.wait()
+
+    @pl.when(upper)
+    def _():
+        normed_out.start()
+        normed_out.wait()
+
+    s.hop_out[:M] = mlp_forward(s, vec_m, mlp_weights).astype(BF16)
     mixed_out.start()
-    normed_out.wait()
-
-    @pl.when(lower)
-    def _():
-        wait_all(merge_saved())
-
-    s.hop_out[:M] = mlp_forward(s, vec_m, mlp_weights).astype(BF16)
     normed_out = deliver_rows(1, 0, s.normed)
-    normed_out.start()
 
     over = range(RELAY // PER)
 
@@ -618,14 +647,34 @@
     def _():
         hop(s.grad_a)
         start_all(hidden_lower)
-        hop_copy(s.grad_a).wait_send()
+        for copy in hop_copies(s.grad_a):
+            copy.wait_send()
         for k in over:
             hidden_over(k, c).start()
-        hop_copy(s.grad_m).wait_recv()
+        normed_out.start()
+        normed_out.wait()
+
+        def bring(at, buffer):
+            back = local(o.tokens.at[at], buffer, s.save_sem.at[at])
+            back.start()
+            back.wait()
+
+        late = [Delivery(0, 8 + k, b, o.hidden.at[k, mine]) for k, b in enumerate((s.normed, s.grad_a))]
+        for k, copy in enumerate(late):
+            bring(k, (s.normed, s.grad_a)[k])
+            copy.start()
+        wait_all(late)
+        bring(4, s.normed)
+        copy = deliver_rows(0, 0, s.normed)
+        copy.start()
+        copy.wait()
+        for copy in hop_copies(s.grad_m):
+            copy.wait_recv()
         grad_m_out.start()
 
     @pl.when(upper)
     def _():
+        normed_out.start()
         start_all(hidden_upper)
         for owner in range(4):
             here, there = output_copy(owner)
@@ -674,12 +723,13 @@
         start_all(right_a_out)
         table_out.start()
         vecs_a_out.start()
-        hop_copy(s.grad_m).wait_send()
+        for copy in hop_copies(s.grad_m):
+            copy.wait_send()
 
     @pl.when(lower)
     def _():
         saved = [
-            local(o.tokens.at[k], s.qkv.at[k], s.out_sem.at[1 + k]) for k in range(2)
+            local(o.tokens.at[2 + k], s.qkv.at[k], s.out_sem.at[1 + k]) for k in range(2)
         ]
         start_all(saved)
         start_all(right_a_out)
@@ -716,7 +766,8 @@
     def _():
         wait_all(right_m_out)
 
-    wait_all(right_a_out + [table_out, vecs_a_out, vecs_m_out, normed_out, mixed_out, grad_m_out])
+    wait_all(right_a_out + [table_out, vecs_a_out, vecs_m_out, mixed_out, grad_m_out])
+    pl.when(upper)(normed_out.wait)
     given = [deliver_rows(0, 0, s.normed), mixed_out, vecs_a_out, grad_a_out] + right_a_out
     given += [normed_out, grad_m_out, vecs_m_out] + right_m_out
     for copy in given:
@@ -797,7 +848,7 @@
         "table": ((HEADS * ROWS, 128), F32),
         "outs": ((2, M, D // 4), BF16),
         "merged": ((4, M, D // 2), BF16),
-        "tokens": ((2, M, D), BF16),
+        "tokens": ((5, M, D), BF16),
     }
     scratch = {
         "w_qkv": pltpu.VMEM((STEPS, D, 3 * GROUP), BF16),
@@ -839,6 +890,7 @@
         "out_sem": DMA((4,)),
         "give_out": DMA((2, 12)),
         "give_in": DMA((2, 12)),
+        "save_sem": DMA((5,)),
         "over_sem": DMA((4,)),
         "over_in": DMA((2, 4)),
         "outs_in": DMA((2,)),
@@ -860,7 +912,7 @@
 
 
 PIECES = 2 * HALF
-AHEAD = 4
+AHEAD = 3
 RING = AHEAD + 2
 LAG = 2
 LEFT = PIECES

time: 310 us -> 297 us (0.958)
  the two profiles are of different devices: /device:TPU:3 before, /device:TPU:7 now
where the time goes in v2:
time: 297 us; the launch traced here: 291 us
  Pallas kernels  290 us (98%)
    pallas_call x1, Pallas kernels, reduce_gradients(): pl.pallas_call(functools.partial(reduce_kernel, bits, tuple(operands)), i...  177 us
    pallas_call x1, Pallas kernels, forward_backward(): pl.pallas_call(functools.partial(main_kernel, tuple(operands), tuple(outs...  108 us

profile of v2, /device:TPU:7, one launch (start us, length us, event | category | flops | bytes accessed | tf_op | source)
XLA Modules:
  0.0 291.3 jit_solution(3561846519091955508)
XLA Ops:
  0.6 107.7 %forward_backward.1 = (bf16[672,1024]{1,0:T(8,128)(2,1)}, bf16[672,1024]{1,0:T(8,128)(2,1)}, bf16[672,1024]{1,0:T(8,128)(2,1)}, bf16[4,672,1024]{2,1,0:T(8,128)(...) custom-call(bf16[3,800,512]{2,1,0:T(8,128)(2,1)} %bitcast.16, ...), custom_call_target="tpu_custom_call" | custom-call | tf_op jit(solution)/shard_map/forward_backward/pallas_call | solution.py:900
  108.3 176.8 %reduce_gradients.1 = (f32[128,4096]{1,0:T(8,128)}, f32[4096,128]{1,0:T(8,128)}, f32[128,128]{1,0:T(8,128)}, bf16[2,336,512]{2,1,0:T(8,128)(2,1)}, f32[2,32,384]{2,1,0:T(8,128)}) custom-call(bf16[672,1024]{1,0:T(8,128)(2,1)} %get-tuple-element.28.refs_0_, bf16[672,1024]{1,0:T(8,128)(2,1)} %get-tuple-element.29.refs_1_, ...), custom_call_target="tpu_custom_call" | custom-call | tf_op jit(solution)/shard_map/reduce_gradients/pallas_call | solution.py:1408
  285.1 5.9 %finish.1 = (bf16[3,200,256]{2,1,0:T(8,128)(2,1)}, f32[3,800,128]{2,1,0:T(8,128)}, f32[128,4096]{1,0:T(8,128)}, f32[4096,128]{1,0:T(8,128)}, f32[3,1,128]{2,1,0:...) custom-call(f32[128,4096]{1,0:T(8,128)} %get-tuple-element.36.first_in, f32[4096,128]{1,0:T(8,128)} %get-tuple-element.37.second_in, ...), custom_call_target="tpu_custom_call" | custom-call | tf_op jit(solution)/shard_map/finish/pallas_call | solution.py:1520

commit v3 on v2

--- a/solution.py
+++ b/solution.py
@@ -1192,6 +1192,7 @@
     def _():
         turn(0, False)
 
+    lax.fori_loop(0, AHEAD, lambda t, _: (send_first(t), 0)[1], 0)
     issue(False)
 
     for index in range(2):
@@ -1203,8 +1204,6 @@
             for target in range(4):
                 if target != index:
                     token_copy(index, target, target).start()
-
-    lax.fori_loop(0, AHEAD, lambda t, _: (send_first(t), 0)[1], 0)
 
     def vec_copy(s):
         width = count >> (s + 1)
@@ -1307,8 +1306,14 @@
             device_id_type=MESH,
         )
 
-    vec_start()
-    table_start()
+    def clear(j, carry):
+        second_ref[pl.ds(pl.multiple_of(j * PIECE, PIECE), PIECE)] = jnp.zeros((PIECE, share), F32)
+        return carry
+
+    lax.fori_loop(by_device(p, (HALF // 2, HALF, 0, HALF)), HALF, clear, 0)
+
+    def sent_by(s):
+        return pieces - 1 + LAG * (bits - 1 - s) - 3
 
     def body(t, carry):
         for s in range(bits):
@@ -1323,15 +1328,24 @@
                     def _():
                         send_first(t + AHEAD)
 
+        for s in range(1, bits):
+            past = t - LAG * s - 3
+
+            @pl.when((past >= 0) & (past < pieces))
+            def _(s=s, past=past):
+                stage_copy(s, past).wait_send()
+
+        pl.when(t == 2)(vec_start)
+        pl.when(t == 4)(table_start)
         for s in range(bits):
 
-            @pl.when(t == 2 * s + 2)
+            @pl.when(t == 2 * s + 4)
             def _(s=s):
                 vec_step(s)
 
         for s in range(bits + 1):
 
-            @pl.when(t == 2 * s + 2)
+            @pl.when(t == 2 * s + 6)
             def _(s=s):
                 table_step(s)
 
@@ -1349,22 +1363,20 @@
 
     lax.fori_loop(0, pieces + LAG * (bits - 1), body, 0)
 
-    def clear(j, carry):
-        second_ref[pl.ds(pl.multiple_of(j * PIECE, PIECE), PIECE)] = jnp.zeros((PIECE, share), F32)
-        return carry
-
-    lax.fori_loop(by_device(p, (HALF // 2, HALF, 0, HALF)), HALF, clear, 0)
-
     def drain(t, carry):
         @pl.when(t >= pieces - RING)
         def _():
             stage_copy(0, t).wait_send()
 
         for s in range(1, bits):
-            stage_copy(s, t).wait_send()
+
+            @pl.when(t > sent_by(s))
+            def _(s=s):
+                stage_copy(s, t).wait_send()
+
         return carry
 
-    lax.fori_loop(0, pieces, drain, 0)
+    lax.fori_loop(pieces - RING, pieces, drain, 0)
     for s in range(bits):
         vec_copy(s).wait_send()
     for s in range(bits + 1):

time: 297 us -> 294 us (0.990)
  the two profiles are of different devices: /device:TPU:7 before, /device:TPU:15 now
where the time goes in v3:
time: 294 us; the launch traced here: 289 us
  Pallas kernels  288 us (98%)
    pallas_call x1, Pallas kernels, reduce_gradients(): pl.pallas_call(functools.partial(reduce_kernel, bits, tuple(operands)), i...  175 us
    pallas_call x1, Pallas kernels, forward_backward(): pl.pallas_call(functools.partial(main_kernel, tuple(operands), tuple(outs...  107 us
    pallas_call x1, Pallas kernels, finish(): pl.pallas_call(finish_kernel, in_specs=[ANYWHERE] * 8, out_specs=[IN_VMEM...  5.9 us

profile of v3, /device:TPU:15, one launch (start us, length us, event | category | flops | bytes accessed | tf_op | source)
XLA Modules:
  0.0 289.1 jit_solution(17276692999445262849)
XLA Ops:
  0.6 106.9 %forward_backward.1 = (bf16[672,1024]{1,0:T(8,128)(2,1)}, bf16[672,1024]{1,0:T(8,128)(2,1)}, bf16[672,1024]{1,0:T(8,128)(2,1)}, bf16[4,672,1024]{2,1,0:T(8,128)(...) custom-call(bf16[3,800,512]{2,1,0:T(8,128)(2,1)} %bitcast.16, ...), custom_call_target="tpu_custom_call" | custom-call | tf_op jit(solution)/shard_map/forward_backward/pallas_call | solution.py:900
  107.5 175.4 %reduce_gradients.1 = (f32[128,4096]{1,0:T(8,128)}, f32[4096,128]{1,0:T(8,128)}, f32[128,128]{1,0:T(8,128)}, bf16[2,336,512]{2,1,0:T(8,128)(2,1)}, f32[2,32,384]{2,1,0:T(8,128)}) custom-call(bf16[672,1024]{1,0:T(8,128)(2,1)} %get-tuple-element.28.refs_0_, bf16[672,1024]{1,0:T(8,128)(2,1)} %get-tuple-element.29.refs_1_, ...), custom_call_target="tpu_custom_call" | custom-call | tf_op jit(solution)/shard_map/reduce_gradients/pallas_call | solution.py:1420
  283.0 5.9 %finish.1 = (bf16[3,200,256]{2,1,0:T(8,128)(2,1)}, f32[3,800,128]{2,1,0:T(8,128)}, f32[128,4096]{1,0:T(8,128)}, f32[4096,128]{1,0:T(8,128)}, f32[3,1,128]{2,1,0:...) custom-call(f32[128,4096]{1,0:T(8,128)} %get-tuple-element.36.first_in, f32[4096,128]{1,0:T(8,128)} %get-tuple-element.37.second_in, ...), custom_call_target="tpu_custom_call" | custom-call | tf_op jit(solution)/shard_map/finish/pallas_call | solution.py:1532

commit v4 on v3

--- a/solution.py
+++ b/solution.py
@@ -390,7 +390,8 @@
     def gifts(parts, got):
         found = []
         for k, (source, target) in enumerate(parts):
-            to = beside[k // 8] if parts is attention_parts and k % 4 == 3 else pair
+            over = k % 4 == 3 if parts is attention_parts else k % 8 in (5, 7)
+            to = beside[k // 8] if over else pair
             found.append(remote(source, target, s.give_sem.at[k], got.at[k], to))
         return found
 

time: 294 us -> 307 us (1.044)
  Pallas kernels: 288 us -> 301 us
    pallas_call x1, Pallas kernels: 107 us -> 120 us  [forward_backward(): pl.pallas_call(functools.partial(main_kernel, tuple(operands), tuple(outs...]
where the time goes in v4:
time: 307 us; the launch traced here: 301 us
  Pallas kernels  301 us (98%)
    pallas_call x1, Pallas kernels, reduce_gradients(): pl.pallas_call(functools.partial(reduce_kernel, bits, tuple(operands)), i...  175 us
    pallas_call x1, Pallas kernels, forward_backward(): pl.pallas_call(functools.partial(main_kernel, tuple(operands), tuple(outs...  120 us

profile of v4, /device:TPU:15, one launch (start us, length us, event | category | flops | bytes accessed | tf_op | source)
XLA Modules:
  0.0 301.5 jit_solution(14598276616901847777)
XLA Ops:
  0.6 119.7 %forward_backward.1 = (bf16[672,1024]{1,0:T(8,128)(2,1)}, bf16[672,1024]{1,0:T(8,128)(2,1)}, bf16[672,1024]{1,0:T(8,128)(2,1)}, bf16[4,672,1024]{2,1,0:T(8,128)(...) custom-call(bf16[3,800,512]{2,1,0:T(8,128)(2,1)} %bitcast.16, ...), custom_call_target="tpu_custom_call" | custom-call | tf_op jit(solution)/shard_map/forward_backward/pallas_call | solution.py:901
  120.3 175.0 %reduce_gradients.1 = (f32[128,4096]{1,0:T(8,128)}, f32[4096,128]{1,0:T(8,128)}, f32[128,128]{1,0:T(8,128)}, bf16[2,336,512]{2,1,0:T(8,128)(2,1)}, f32[2,32,384]{2,1,0:T(8,128)}) custom-call(bf16[672,1024]{1,0:T(8,128)(2,1)} %get-tuple-element.28.refs_0_, bf16[672,1024]{1,0:T(8,128)(2,1)} %get-tuple-element.29.refs_1_, ...), custom_call_target="tpu_custom_call" | custom-call | tf_op jit(solution)/shard_map/reduce_gradients/pallas_call | solution.py:1421
  295.4 5.9 %finish.1 = (bf16[3,200,256]{2,1,0:T(8,128)(2,1)}, f32[3,800,128]{2,1,0:T(8,128)}, f32[128,4096]{1,0:T(8,128)}, f32[4096,128]{1,0:T(8,128)}, f32[3,1,128]{2,1,0:...) custom-call(f32[128,4096]{1,0:T(8,128)} %get-tuple-element.36.first_in, f32[4096,128]{1,0:T(8,128)} %get-tuple-element.37.second_in, ...), custom_call_target="tpu_custom_call" | custom-call | tf_op jit(solution)/shard_map/finish/pallas_call | solution.py:1533
